TPU v7x, 32 devices: a whole 2x2x4 slice. The times are simulated.
32 devices in a mesh: grp: 1, rows: 32 (over z, y, x, core).
Axes of the slice: x: 2, y: 2, z: 4, core: 2. Of those that a mesh axis runs over, the one named last changes fastest.
Arguments:
- embeddings: bfloat16 [16384, 1024], P(('grp', 'rows')), may hold values from -30 to 30
- centroids: bfloat16 [4096, 1024], replicated, may hold values from -0.1875 to 0.1875
- log_weights: float32 [4096], replicated, may hold values from -1 to 1
Outputs:
- new_centroids: bfloat16 [4096, 1024], P(('grp', 'rows'))
- new_log_weights: float32 [4096], P(('grp', 'rows'))
- log_normalizer: float32 [16384], P(('grp', 'rows'))
All inputs are finite; a program needn't handle non-finite values.
Results may differ from a plain program's by a relative error of at most 0.0034.
Values may be sent and summed in bfloat16 or wider, within the bound.
No kernel may reach another device: no remote copies, remote signals or barrier semaphores. Data moves between devices by JAX's collectives and lax.ppermute only.
A program may use at most 128 MiB of HBM per device.

v0:
```python
import jax
import jax.numpy as jnp
from jax import lax
from jax.sharding import PartitionSpec as P

KAPPA = 32


def local(embeddings, centroids, log_weights):
    embed_float = embeddings.astype(jnp.float32)
    unit_rows = (
        embed_float * lax.rsqrt(jnp.sum(embed_float * embed_float, 1, keepdims=True) + 1e-06)
    ).astype(jnp.bfloat16)
    scores = (
        KAPPA * jnp.dot(unit_rows, centroids.T, preferred_element_type=jnp.float32) + log_weights
    )
    exponent = jnp.exp(scores)
    responsible = (exponent / jnp.sum(exponent, 1, keepdims=True)).astype(jnp.bfloat16)
    counts = lax.psum(jnp.sum(responsible.astype(jnp.float32), 0), "rows")
    row_total = unit_rows.shape[0] * lax.axis_size("rows")
    new_log_weights = jnp.log(counts / row_total)
    term_sums = jnp.dot(responsible.T, unit_rows, preferred_element_type=jnp.float32)
    comp_dev = centroids.shape[0] // lax.axis_size("rows")
    own_start = lax.axis_index("rows") * comp_dev
    own_log_weights = lax.dynamic_slice_in_dim(new_log_weights, own_start, comp_dev)
    own_sums = lax.psum_scatter(term_sums, "rows", scatter_dimension=0, tiled=True)
    directions = (
        own_sums * lax.rsqrt(jnp.sum(own_sums * own_sums, 1, keepdims=True) + 1e-06)
    ).astype(jnp.bfloat16)
    block_scores = (
        KAPPA
        * jnp.dot(
            unit_rows,
            lax.all_gather(directions, "rows", axis=0, tiled=True).T,
            preferred_element_type=jnp.float32,
        )
        + new_log_weights
    )
    exp_total = jnp.sum(jnp.exp(block_scores), 1)
    return (directions, own_log_weights, jnp.log(exp_total))


def solution(mesh):
    return jax.shard_map(
        local,
        mesh=mesh,
        in_specs=(P(("grp", "rows"), None), P(), P()),
        out_specs=(P(("grp", "rows"), None), P(("grp", "rows")), P(("grp", "rows"))),
        check_vma=False,
    )
```

profile of v0, /device:TPU:0, one launch (start us, length us, event | category | flops | bytes accessed | tf_op | source)
XLA Modules:
  0.0 313.0 jit_solution(6081287427242209415)
XLA Ops:
  7.2 0.0 reduce-scatter.2.cloned.1.call-start
  7.2 1.5 fusion.1
  8.7 0.0 copy-start.1
  8.7 8.8 %fusion = (f32[512]{0:T(512)S(1)}, f32[512,4096]{1,0:T(8,128)S(1)}) fusion(f32[4096]{0:T(1024)} %param.5, bf16[4096,1024]{1,0:T(8,128)(2,1)} %param.4, bf16[512,1024]{1,0:T(8,128)(2,1)} %param.3, f32[512]{0:T(512)S(1)} %add_rsqrt_fusion), kind=kOutput, calls=%fused_computation.4 | convolution fusion | flops 4302831104 | bytes 17846272 | tf_op jit(solution)/shard_map/dot_general | solution.py:15
  17.5 0.0 copy-start
  17.5 0.0 copy-done.1
  17.5 2.1 convert_reduce_fusion
  19.7 0.0 copy-done
  19.7 8.3 %fusion.4 = f32[4096,1024]{1,0:T(8,128)} fusion(bf16[512,4096]{1,0:T(8,128)(2,1)S(1)} %get-tuple-element.4, bf16[512,1024]{1,0:T(8,128)(2,1)S(1)} %copy-done, f32[512]{0:T(512)S(1)} %add_rsqrt_fusion), kind=kOutput, calls=%fused_computation.14 | convolution fusion | flops 4296540160 | bytes 22022144 | tf_op jit(solution)/shard_map/dot_general | solution.py:22
  28.0 0.0 reduce-scatter.2.cloned.1.call-update
  28.0 0.0 all-gather.2.cloned.1.call-start
  28.1 185.7 %reduce-scatter.2.cloned.1.call-done = f32[128,1024]{1,0:T(8,128)} async-done(((f32[4096,1024]{1,0:T(8,128)}), f32[128,1024]{1,0:T(8,128)}) %reduce-scatter.2.cloned.1.call-update) | async-done | bytes 524304 | tf_op jit(solution)/shard_map/reduce_scatter | solution.py:26
  213.8 1.2 multiply_reduce_fusion
  214.9 1.8 multiply_convert_fusion
  216.8 0.0 all-gather.2.cloned.1.call-update
  216.8 42.9 %psum.7 = f32[4096]{0:T(1024)S(1)} all-reduce(f32[4096]{0:T(1024)S(1)} %get-tuple-element.3), channel_id=1, replica_groups=mesh['grp'=1,'rows'=32] {'rows'}, use_global_device_ids=true, to_apply=%region_5.0 | all-reduce | flops 4096 | bytes 32768 | tf_op jit(solution)/shard_map/psum | solution.py:19
  259.7 0.6 dynamic_slice.3
  260.3 36.2 %all-gather.2.cloned.1.call-done = bf16[4096,1024]{1,0:T(8,128)(2,1)} async-done(((bf16[128,1024]{1,0:T(8,128)(2,1)}), bf16[4096,1024]{1,0:T(8,128)(2,1)}) %all-gather.2.cloned.1.call-update) | async-done | bytes 8388624 | tf_op jit(solution)/shard_map/all_gather | solution.py:34
  296.5 9.1 %exponential_reduce_fusion = f32[512]{0:T(512)S(1)} fusion(bf16[4096,1024]{1,0:T(8,128)(2,1)} %all-gather.2.cloned.1.call-done, f32[4096]{0:T(1024)S(1)} %multiply_log_fusion, bf16[512,1024]{1,0:T(8,128)(2,1)S(1)} %copy-done, f32[512]{0:T(512)S(1)} %add_rsqrt_fusion), kind=kOutput, calls=%fused_computation | convolution fusion | flops 4302831104 | bytes 9457664 | tf_op jit(solution)/shard_map/dot_general | solution.py:32
  305.5 0.6 log.7
  (3 shorter events, 0.0 us)
Async XLA Ops:
  7.2 206.6 %reduce-scatter.2.cloned.1.call-start = ((), (), s32[]{:S(2)}) async-start(), calls=%async_computation.1 | async-start | bytes 17301504 | tf_op jit(solution)/shard_map/reduce_scatter | solution.py:26
  8.7 8.8 %copy-start.1 = (f32[4096]{0:T(1024)S(1)}, f32[4096]{0:T(1024)}, u32[]{:S(2)}) copy-start(f32[4096]{0:T(1024)} %param.5) | copy-start | bytes 49156
  17.5 2.1 copy-start
  28.0 268.5 %all-gather.2.cloned.1.call-start = ((), (), s32[]{:S(2)}) async-start(), calls=%async_computation.2 | async-start | bytes 8650752 | tf_op jit(solution)/shard_map/all_gather | solution.py:34
Sparse Core Ops, SparseCore 0:
  28.1 185.5 reduce-scatter.1
  217.2 79.2 all-gather.1
where the time goes:
time: 313 us
  waiting for transfers between devices  222 us (71%)
  blocking collectives  42.9 us (14%)
  matrix products  26.2 us (8%)
  between operations  14.1 us (5%)
  other arithmetic  6.64 us (2%)
    reduce_scatter x1, waiting for transfers between devices, local(): lax.psum_scatter(term_sums, 'rows', scatter_dimension=0, tiled=True)  186 us
    psum x1, blocking collectives, local(): counts = lax.psum(jnp.sum(responsible.astype(jnp.float32), 0), 'rows')  42.9 us
    all_gather x1, waiting for transfers between devices, local(): lax.all_gather(directions, 'rows', axis=0, tiled=True)  36.2 us
    dot_general x1, matrix products, local(): jnp.dot(unit_rows, lax.all_gather(directions, 'rows', axis=0, tiled=True)...  9.07 us
    dot_general x1, matrix products, local(): jnp.dot(unit_rows, centroids.T, preferred_element_type=jnp.float32)  8.77 us
    dot_general x1, matrix products, local(): jnp.dot(responsible.T, unit_rows, preferred_element_type=jnp.float32)  8.32 us
  transfers between devices with their start and end apart: 2, of which 2 were waited for; matrix products, arithmetic and copies ran while one was open for 0% of the time, Pallas kernels for 0%

commit v1 on v0

v1 whole, which is shorter than its diff:
```python
import functools

import jax
import jax.numpy as jnp
from jax import lax
from jax.experimental import pallas as pl
from jax.experimental.pallas import tpu as pltpu
from jax.sharding import PartitionSpec as P

KAPPA = 32
EPS = 1e-06
LANES = 128
CORE, ACROSS, ALONG = 0, 1, 3
MIB = 1 << 20
F32, BF16 = jnp.float32, jnp.bfloat16
VMEM = pl.BlockSpec(memory_space=pltpu.VMEM)


def params(mib):
    return pltpu.CompilerParams(vmem_limit_bytes=mib * MIB)


def cost(macs, nbytes, exps=0):
    return pl.CostEstimate(flops=2 * macs, bytes_accessed=nbytes, transcendentals=exps)


def column(row):
    return jnp.broadcast_to(row, (LANES, row.shape[1])).T


def nt_dot(a, b):
    return lax.dot_general(a, b, (((1,), (1,)), ((), ())), preferred_element_type=F32)


def exp_scores(comps, rows, shift):
    dots = nt_dot(comps, rows)
    return [
        jnp.exp(KAPPA * dots[:, j : j + LANES] + shift) for j in range(0, dots.shape[1], LANES)
    ]


def unit_kernel(e_ref, a_ref, b_ref):
    half = a_ref.shape[0]
    for i, out in enumerate((a_ref, b_ref)):
        x = e_ref[i * half : (i + 1) * half, :].astype(F32)
        out[...] = (x * lax.rsqrt(jnp.sum(x * x, 1, keepdims=True) + EPS)).astype(BF16)


def unit(emb):
    rows, dim = emb.shape
    half = jax.ShapeDtypeStruct((rows // 2, dim), BF16)
    return pl.pallas_call(
        unit_kernel,
        out_shape=(half, half),
        in_specs=[VMEM],
        out_specs=(VMEM, VMEM),
        compiler_params=params(24),
        cost_estimate=cost(0, 4 * rows * dim, rows),
        name="unit_rows",
    )(emb)


def denom_kernel(c_ref, lw_ref, a_ref, b_ref, out_ref):
    @pl.when(pl.program_id(0) == 0)
    def _():
        out_ref[...] = jnp.zeros_like(out_ref)

    shift = column(lw_ref[0])
    half = a_ref.shape[0]
    for i, rows in enumerate((a_ref, b_ref)):
        pieces = exp_scores(c_ref[...], rows[...], shift)
        out_ref[:, i * half : (i + 1) * half] += jnp.concatenate(
            [jnp.sum(p, 0, keepdims=True) for p in pieces], 1
        )

    @pl.when(pl.program_id(0) == pl.num_programs(0) - 1)
    def _():
        out_ref[...] = 1.0 / out_ref[...]


def denominators(cen, lw, ua, ub):
    comps, dim = cen.shape
    half = ua.shape[0]
    tile = min(512, comps)
    whole = lambda shape: pl.BlockSpec(shape, lambda i: (0,) * len(shape))
    return pl.pallas_call(
        denom_kernel,
        grid=(comps // tile,),
        out_shape=jax.ShapeDtypeStruct((1, 2 * half), F32),
        in_specs=[
            pl.BlockSpec((tile, dim), lambda i: (i, 0)),
            pl.BlockSpec((1, 1, tile), lambda i: (i, 0, 0)),
            whole((half, dim)),
            whole((half, dim)),
        ],
        out_specs=whole((1, 2 * half)),
        compiler_params=params(24),
        cost_estimate=cost(2 * half * comps * dim, 2 * (comps + 2 * half) * dim, 2 * half * comps),
        name="denominators",
    )(cen, lw.reshape(comps // tile, 1, tile), ua, ub)


def sums_kernel(first, last, c_ref, lw_ref, inv_ref, *refs):
    pieces, refs = refs[:4], refs[4:]
    if not first:
        acc_in, cnt_in, refs = refs[0], refs[1], refs[2:]
    if last:
        keep_ref, send_ref, counts_ref, acc, cnt = refs
    else:
        acc, cnt = refs
    shift = column(lw_ref[...])
    half = pieces[0].shape[0]
    count = None
    total = None
    for i, piece in enumerate(pieces):
        u = piece[...]
        inv = inv_ref[i // 2 : i // 2 + 1, (i % 2) * half : (i % 2 + 1) * half]
        resp = []
        for j, e in enumerate(exp_scores(c_ref[...], u, shift)):
            r = (e * inv[:, j * LANES : (j + 1) * LANES]).astype(BF16)
            r32 = r.astype(F32)
            count = r32 if count is None else count + r32
            resp.append(r)
        part = jnp.dot(jnp.concatenate(resp, 1), u, preferred_element_type=F32)
        if i == 0:
            acc[...] = part if first else acc_in[...] + part
        else:
            acc[...] += part
    cnt[...] = count if first else cnt_in[...] + count
    if last:
        near = keep_ref.shape[0]
        keep_ref[...] = acc[:near, :]
        send_ref[...] = acc[near:, :].astype(BF16)
        counts_ref[...] = jnp.sum(cnt[...].T, 0, keepdims=True)


def sums(cen, lw, inv, pieces, state, last):
    comps, dim = cen.shape
    rows = 4 * pieces[0].shape[0]
    first = state is None
    acc = jax.ShapeDtypeStruct((comps, dim), F32)
    cnt = jax.ShapeDtypeStruct((comps, LANES), F32)
    if last:
        out_shape = (
            jax.ShapeDtypeStruct((comps // 2, dim), F32),
            jax.ShapeDtypeStruct((comps // 2, dim), BF16),
            jax.ShapeDtypeStruct((1, comps), F32),
        )
        scratch = [pltpu.VMEM(acc.shape, F32), pltpu.VMEM(cnt.shape, F32)]
    else:
        out_shape, scratch = (acc, cnt), []
    args = [cen, lw, inv, *pieces] + ([] if first else list(state))
    aliases = {} if first or last else {len(args) - 2: 0, len(args) - 1: 1}
    return pl.pallas_call(
        functools.partial(sums_kernel, first, last),
        out_shape=out_shape,
        in_specs=[VMEM] * len(args),
        out_specs=(VMEM,) * len(out_shape),
        scratch_shapes=scratch,
        input_output_aliases=aliases,
        compiler_params=params(24),
        cost_estimate=cost(2 * rows * comps * dim, 2 * (comps + rows) * dim, rows * comps),
        name="sums",
    )(*args)


def directions_kernel(keep_ref, *refs):
    total = keep_ref[...]
    for ref in refs[:-1]:
        total = total + ref[...].astype(F32)
    refs[-1][...] = (total * lax.rsqrt(jnp.sum(total * total, 1, keepdims=True) + EPS)).astype(BF16)


def directions(keep, received):
    return pl.pallas_call(
        directions_kernel,
        out_shape=jax.ShapeDtypeStruct(keep.shape, BF16),
        in_specs=[VMEM] * (1 + len(received)),
        out_specs=VMEM,
        compiler_params=params(24),
        cost_estimate=cost(0, 10 * keep.size, keep.shape[0]),
        name="directions",
    )(keep, *received)


def normalizer_kernel(n_comps, first, *refs):
    comps, refs = refs[:n_comps], refs[n_comps:]
    lw_ref, refs = refs[0], refs[1:]
    before, refs = (None, refs) if first else (refs[0], refs[1:])
    pieces, out_ref = refs[:-1], refs[-1]
    c = jnp.concatenate([r[...] for r in comps], 0)
    shift = column(lw_ref[...])
    half = pieces[0].shape[0]
    for i, piece in enumerate(pieces):
        s = jnp.concatenate(
            [jnp.sum(p, 0, keepdims=True) for p in exp_scores(c, piece[...], shift)], 1
        )
        at = slice(i // 2, i // 2 + 1), slice((i % 2) * half, (i % 2 + 1) * half)
        out_ref[at] = s if first else before[at] + s


def normalizers(comps, lw, before, pieces):
    half, dim = pieces[0].shape
    n_comps, rows = sum(c.shape[0] for c in comps), len(pieces) * half
    args = [*comps, lw] + ([] if before is None else [before]) + list(pieces)
    return pl.pallas_call(
        functools.partial(normalizer_kernel, len(comps), before is None),
        out_shape=jax.ShapeDtypeStruct((len(pieces) // 2, 2 * half), F32),
        in_specs=[VMEM] * len(args),
        out_specs=VMEM,
        compiler_params=params(32),
        cost_estimate=cost(rows * n_comps * dim, 2 * (n_comps + rows) * dim, rows * n_comps),
        name="normalizers",
    )(*args)


def local(embeddings, centroids, log_weights):
    n = lax.axis_size("rows")
    comps, dim = centroids.shape
    block = comps // n
    row_total = embeddings.shape[0] * n
    me = lax.axis_index("rows")
    group_bits = (CORE, ACROSS, ALONG)
    core, across, along = (1 << b for b in group_bits)
    far = [1 << b for b in range(n.bit_length() - 1) if b not in group_bits]

    def swap(x, mask):
        return lax.ppermute(x, "rows", [(i, i ^ mask) for i in range(n)])

    offsets = [0]
    for mask in reversed(far):
        offsets = offsets + [o | mask for o in offsets]
    offsets = sorted(offsets, key=lambda o: [bool(o & m) for m in far])
    where = {o: q for q, o in enumerate(offsets)}
    starts = [(me ^ o) * block for o in offsets]
    cen = jnp.concatenate([lax.dynamic_slice_in_dim(centroids, s, block) for s in starts])
    lw = jnp.concatenate([lax.dynamic_slice_in_dim(log_weights, s, block) for s in starts])
    lw = lw[None]

    ua, ub = unit(embeddings)
    xb, za = swap(ub, across), swap(ua, along)
    xa, zb = swap(ua, across), swap(ub, along)
    own_pair = (ua, ub, swap(ua, core), swap(ub, core))
    inv = denominators(centroids, log_weights, ua, ub)
    inv = jnp.concatenate([inv, swap(inv, core)])
    inv_x, inv_z = swap(inv, across), swap(inv, along)
    da, db = swap(za, across), swap(xb, along)
    inv_d = swap(inv_z, across)
    x_pair = (xa, xb, swap(xa, core), swap(xb, core))
    z_pair = (za, zb, swap(za, core), swap(zb, core))
    d_pair = (da, db, swap(da, core), swap(db, core))

    state = sums(cen, lw, inv, own_pair, None, False)
    state = sums(cen, lw, inv_x, x_pair, state, False)
    state = sums(cen, lw, inv_z, z_pair, state, False)
    keep, send, counts = sums(cen, lw, inv_d, d_pair, state, True)

    counts = counts.reshape(len(offsets), block)
    for mask in far:
        order = [where[o ^ mask] for o in offsets]
        got = swap(counts, mask)
        counts = counts + jnp.concatenate([got[q : q + 1] for q in order])
    new_lw = jnp.log(counts / row_total)
    own_lw = new_lw[0]

    def rows_of(x, q):
        return x[q * block : (q + 1) * block]

    half = len(offsets) // 2
    parts = {o: [rows_of(keep, q)] for q, o in enumerate(offsets[:half])}
    sent = {o: rows_of(send, q) for q, o in enumerate(offsets[half:])}
    for k, mask in enumerate(far):
        leaving = [o for o in offsets if o & mask and not any(o & m for m in far[:k])]
        for o in reversed(leaving):
            x = sent[o] if k == 0 else sum(p.astype(F32) for p in parts.pop(o)).astype(BF16)
            parts[o ^ mask].append(swap(x, mask))
    own_dirs = directions(parts[0][0], parts[0][1:])

    dirs = {0: own_dirs}
    for mask in reversed(far):
        for o in list(dirs):
            dirs[o | mask] = swap(dirs[o], mask)
    pieces = own_pair + x_pair + z_pair + d_pair
    block_lw = lambda os: jnp.concatenate([new_lw[where[o]] for o in os])[None]
    early = [o for o in offsets if o in (0, far[0])]
    late = [o for o in offsets if o not in early]
    total = normalizers([dirs[o] for o in early], block_lw(early), None, pieces)
    total = normalizers([dirs[o] for o in late], block_lw(late), total, pieces)

    for mask in (along, across, core):
        stay = total.shape[0] // 2
        total = total[:stay] + swap(total[stay:], mask)
    return own_dirs, own_lw, jnp.log(total[0])


def solution(mesh):
    return jax.shard_map(
        local,
        mesh=mesh,
        in_specs=(P(("grp", "rows"), None), P(), P()),
        out_specs=(P(("grp", "rows"), None), P(("grp", "rows")), P(("grp", "rows"))),
        check_vma=False,
    )
```

time: 313 us -> 128 us (0.41)
  waiting for transfers between devices: 222 us -> 61.4 us
  blocking collectives: 42.9 us -> 0 us
  Pallas kernels: 0 us -> 31.9 us
  matrix products: 26.2 us -> 0 us
  starting transfers between devices: 0.08 us -> 23.8 us
  between operations: 14.1 us -> 0.84 us
  local copies, waits for them, and re-layouts: 1.2 us -> 8.45 us
  other arithmetic: 6.64 us -> 0.83 us
    reduce_scatter x1 -> x0, waiting for transfers between devices: 186 us -> none  [local(): lax.psum_scatter(term_sums, 'rows', scatter_dimension=0, tiled=True)]
    ppermute x0 -> x29, waiting for transfers between devices: none -> 61.4 us  [swap(): return lax.ppermute(x, 'rows', [(i, i ^ mask) for i in range(n)])]
    psum x1 -> x0, blocking collectives: 42.9 us -> none  [local(): counts = lax.psum(jnp.sum(responsible.astype(jnp.float32), 0), 'rows')]
    all_gather x1 -> x0, waiting for transfers between devices: 36.2 us -> none  [local(): lax.all_gather(directions, 'rows', axis=0, tiled=True)]
    pallas_call x0 -> x9, Pallas kernels: none -> 31.9 us  [the longest x4 15.5 us: sums(): pl.pallas_call(functools.partial(sums_kernel, first, last), out_shape=out...]
    dot_general x3 -> x0, matrix products: 26.2 us -> none  [the longest x1 9.07 us: local(): jnp.dot(unit_rows, lax.all_gather(directions, 'rows', axis=0, tiled=True)...]
    ppermute x0 -> x29, starting transfers between devices: none -> 23.8 us  [swap(): return lax.ppermute(x, 'rows', [(i, i ^ mask) for i in range(n)])]
    unnamed x4 -> x10, local copies, waits for them, and re-layouts: 0.01 us -> 6.26 us
  transfers between devices with their start and end apart: 2 -> 29, of which waited for: 2 -> 15; matrix products, arithmetic and copies ran while one was open for 0% -> 2% of each run, Pallas kernels for 0% -> 17%
where the time goes in v1:
time: 128 us; the launch traced here: 127 us
  waiting for transfers between devices  61.4 us (48%)
  Pallas kernels  31.9 us (25%)
  starting transfers between devices  23.8 us (19%)
  local copies, waits for them, and re-layouts  8.45 us (7%)
    ppermute x29, waiting for transfers between devices, swap(): return lax.ppermute(x, 'rows', [(i, i ^ mask) for i in range(n)])  61.4 us
    ppermute x29, starting transfers between devices, swap(): return lax.ppermute(x, 'rows', [(i, i ^ mask) for i in range(n)])  23.8 us
    pallas_call x4, Pallas kernels, sums(): pl.pallas_call(functools.partial(sums_kernel, first, last), out_shape=out...  15.5 us
    pallas_call x2, Pallas kernels, normalizers(): pl.pallas_call(functools.partial(normalizer_kernel, len(comps), before is...  8.76 us
    pallas_call x1, Pallas kernels, denominators(): pl.pallas_call(denom_kernel, grid=(comps // tile,), out_shape=jax.ShapeDt...  6.48 us
    unnamed x10, local copies, waits for them, and re-layouts  6.26 us
  transfers between devices with their start and end apart: 29, of which 15 were waited for; matrix products, arithmetic and copies ran while one was open for 2% of the time, Pallas kernels for 17%

profile of v1, /device:TPU:0, one launch (start us, length us, event | category | flops | bytes accessed | tf_op | source)
XLA Modules:
  0.0 127.3 jit_solution(10493379976332191321)
XLA Ops:
  2.7 2.6 %collective-permute-start.5 = (bf16[256,1024]{1,0:T(8,128)(2,1)S(1)}, bf16[256,1024]{1,0:T(8,128)(2,1)S(1)}, u32[]{:S(2)}, u32[]{:S(2)}) collective-permute-start(bf16[256,1024]{1,0:T(8,128)(2,1)S(1)} %get-tuple-element.15.b_ref.refs_1_.refs_4_.refs_5_), channel_id=1, source_target_pairs={{0,2},{1,3},{2,0},{3,1},{4,6},{5,7},{6,4},{7,5},{8,10},{9,11},{10,... | collective-permute-start | bytes 1572872 | tf_op jit(solution)/shard_map/ppermute | solution.py:228
  7.0 3.4 %copy-done.2 = bf16[4096,1024]{1,0:T(8,128)(2,1)S(1)} copy-done((bf16[4096,1024]{1,0:T(8,128)(2,1)S(1)}, bf16[4096,1024]{1,0:T(8,128)(2,1)}, u32[]{:S(2)}) %copy-start.2) | copy-done | bytes 8388632
  11.1 6.5 %denominators.1 = f32[1,512]{1,0:T(1,128)S(1)} custom-call(bf16[4096,1024]{1,0:T(8,128)(2,1)S(1)} %copy-done.2, f32[8,1,512]{2,1,0:T(1,128)S(1)} %bitcast.22, bf16[256,1024]{1,0:T(8,128)(2,1)S(1)} %get-tuple-element.14.a_ref.refs_0_.refs_3_.refs_4_, bf16[256,1024]{1,0:T(8,128)(2,1)S(1)} %get-tuple-element.15.b_ref.refs_1_.refs_4_.refs_5_), custom_call_target="tpu_custom_call" | custom-call | flops 4294967296 | bytes 9437184 | tf_op jit(solution)/shard_map/denominators/pallas_call | solution.py:86
  19.4 3.1 %collective-permute-done.12.inv_ref = f32[2,512]{1,0:T(2,128)S(1)} collective-permute-done((f32[2,512]{1,0:T(2,128)S(1)}, f32[2,512]{1,0:T(2,128)S(1)}, u32[]{:S(2)}, u32[]{:S(2)}) %collective-permute-start.12) | collective-permute-done | bytes 4128 | tf_op jit(solution)/shard_map/ppermute | solution.py:228
  22.9 3.2 %collective-permute-done.1.inv_ref = f32[2,512]{1,0:T(2,128)S(1)} collective-permute-done((f32[2,512]{1,0:T(2,128)S(1)}, f32[2,512]{1,0:T(2,128)S(1)}, u32[]{:S(2)}, u32[]{:S(2)}) %collective-permute-start.1) | collective-permute-done | bytes 4128 | tf_op jit(solution)/shard_map/ppermute | solution.py:228
  26.8 1.8 %collective-permute-start.4 = (bf16[256,1024]{1,0:T(8,128)(2,1)S(1)}, bf16[256,1024]{1,0:T(8,128)(2,1)}, u32[]{:S(2)}, u32[]{:S(2)}) collective-permute-start(bf16[256,1024]{1,0:T(8,128)(2,1)S(1)} %collective-permute-done.3.refs_0_.refs_11_.refs_12_), channel_id=1, source_target_pairs={{0,2},{1,3},{2,0},{3,1},{4,6},{5,7},{6,4},{7,5},{8,10},{9,11},{10,... | collective-permute-start | bytes 1572872 | tf_op jit(solution)/shard_map/ppermute | solution.py:228
  28.6 1.6 %collective-permute-start.6 = (bf16[256,1024]{1,0:T(8,128)(2,1)S(1)}, bf16[256,1024]{1,0:T(8,128)(2,1)}, u32[]{:S(2)}, u32[]{:S(2)}) collective-permute-start(bf16[256,1024]{1,0:T(8,128)(2,1)S(1)} %collective-permute-done.5.refs_1_.refs_8_.refs_9_), channel_id=1, source_target_pairs={{0,8},{1,9},{2,10},{3,11},{4,12},{5,13},{6,14},{7,15},{8,0},{9,1},... | collective-permute-start | bytes 1572872 | tf_op jit(solution)/shard_map/ppermute | solution.py:228
  31.5 9.5 %collective-permute-done.13.refs_0_.refs_7_.refs_8_ = bf16[256,1024]{1,0:T(8,128)(2,1)} collective-permute-done((bf16[256,1024]{1,0:T(8,128)(2,1)S(1)}, bf16[256,1024]{1,0:T(8,128)(2,1)}, u32[]{:S(2)}, u32[]{:S(2)}) %collective-permute-start.13) | collective-permute-done | bytes 524320 | tf_op jit(solution)/shard_map/ppermute | solution.py:228
  43.0 6.2 %collective-permute-done.4.refs_0_.refs_15_.refs_16_ = bf16[256,1024]{1,0:T(8,128)(2,1)} collective-permute-done((bf16[256,1024]{1,0:T(8,128)(2,1)S(1)}, bf16[256,1024]{1,0:T(8,128)(2,1)}, u32[]{:S(2)}, u32[]{:S(2)}) %collective-permute-start.4) | collective-permute-done | bytes 524320 | tf_op jit(solution)/shard_map/ppermute | solution.py:228
  49.6 2.9 %sums.4 = (f32[512,1024]{1,0:T(8,128)S(1)}, f32[512,128]{1,0:T(8,128)S(1)}) custom-call(bf16[512,1024]{1,0:T(8,128)(2,1)S(1)} %pad_maximum_fusion.c_ref, f32[1,512]{1,0:T(1,128)S(1)} %bitcast.18, f32[2,512]{1,0:T(2,128)S(1)} %pad_maximum_fusion.1.inv_ref, bf16[256,1024]{1,0:T(8,128)(2,1)S(1)} %get-tuple-element.14.a_ref.refs_0_.refs_3_.refs_4_, ...), custom_call_target="tpu_custom_call" | custom-call | flops 2147483648 | bytes 3145728 | tf_op jit(solution)/shard_map/sums/pallas_call | solution.py:154
  53.9 4.3 %sums.5 = (f32[512,1024]{1,0:T(8,128)S(1)}, f32[512,128]{1,0:T(8,128)S(1)}) custom-call(bf16[512,1024]{1,0:T(8,128)(2,1)S(1)} %pad_maximum_fusion.c_ref, f32[1,512]{1,0:T(1,128)S(1)} %bitcast.19, f32[2,512]{1,0:T(2,128)S(1)} %collective-permute-done.12.inv_ref, ...), custom_call_target="tpu_custom_call", output_to_operand_aliasing={{0}: (7, {}), {1}: (8, {})} | custom-call | flops 2147483648 | bytes 3145728 | tf_op jit(solution)/shard_map/sums/pallas_call | solution.py:154
  58.2 4.1 %sums.6 = (f32[512,1024]{1,0:T(8,128)S(1)}, f32[512,128]{1,0:T(8,128)S(1)}) custom-call(bf16[512,1024]{1,0:T(8,128)(2,1)S(1)} %pad_maximum_fusion.c_ref, f32[1,512]{1,0:T(1,128)S(1)} %bitcast.20, f32[2,512]{1,0:T(2,128)S(1)} %collective-permute-done.1.inv_ref, ...), custom_call_target="tpu_custom_call", output_to_operand_aliasing={{0}: (7, {}), {1}: (8, {})} | custom-call | flops 2147483648 | bytes 3145728 | tf_op jit(solution)/shard_map/sums/pallas_call | solution.py:154
  62.3 4.2 %sums.7 = (f32[256,1024]{1,0:T(8,128)S(1)}, bf16[256,1024]{1,0:T(8,128)(2,1)S(1)}, f32[1,512]{1,0:T(1,128)S(1)}) custom-call(bf16[512,1024]{1,0:T(8,128)(2,1)S(1)} %pad_maximum_fusion.c_ref, f32[1,512]{1,0:T(1,128)S(1)} %bitcast.21, f32[2,512]{1,0:T(2,128)S(1)} %collective-permute-done.2.inv_ref, ...), custom_call_target="tpu_custom_call" | custom-call | flops 2147483648 | bytes 3145728 | tf_op jit(solution)/shard_map/sums/pallas_call | solution.py:154
  66.5 1.6 %collective-permute-start.21 = (f32[4,128]{1,0:T(4,128)S(1)}, f32[4,128]{1,0:T(4,128)S(1)}, u32[]{:S(2)}, u32[]{:S(2)}) collective-permute-start(f32[4,128]{1,0:T(4,128)S(1)} %bitcast.16), channel_id=1, source_target_pairs={{0,4},{1,5},{2,6},{3,7},{4,0},{5,1},{6,2},{7,3},{8,12},{9,13},{10,... | collective-permute-start | bytes 6152 | tf_op jit(solution)/shard_map/ppermute | solution.py:228
  70.4 2.6 %collective-permute-start.22 = (f32[4,128]{1,0:T(4,128)S(1)}, f32[4,128]{1,0:T(4,128)S(1)}, u32[]{:S(2)}, u32[]{:S(2)}) collective-permute-start(f32[4,128]{1,0:T(4,128)S(1)} %maximum_add_fusion), channel_id=1, source_target_pairs={{0,16},{1,17},{2,18},{3,19},{4,20},{5,21},{6,22},{7,23},{8,24},{9,... | collective-permute-start | bytes 6152 | tf_op jit(solution)/shard_map/ppermute | solution.py:228
  73.1 4.5 %collective-permute-done.19 = bf16[128,1024]{1,0:T(8,128)(2,1)S(1)} collective-permute-done((bf16[128,1024]{1,0:T(8,128)(2,1)S(1)}, bf16[128,1024]{1,0:T(8,128)(2,1)S(1)}, u32[]{:S(2)}, u32[]{:S(2)}) %collective-permute-start.19) | collective-permute-done | bytes 262176 | tf_op jit(solution)/shard_map/ppermute | solution.py:228
  77.7 2.6 %collective-permute-start.20 = (bf16[128,1024]{1,0:T(8,128)(2,1)S(1)}, bf16[128,1024]{1,0:T(8,128)(2,1)S(1)}, u32[]{:S(2)}, u32[]{:S(2)}) collective-permute-start(bf16[128,1024]{1,0:T(8,128)(2,1)S(1)} %get-tuple-element.29), channel_id=1, source_target_pairs={{0,16},{1,17},{2,18},{3,19},{4,20},{5,21},{6,22},{7,23},{8,24},{9,... | collective-permute-start | bytes 786440 | tf_op jit(solution)/shard_map/ppermute | solution.py:228
  80.3 1.8 %collective-permute-done.18.refs_0_ = bf16[128,1024]{1,0:T(8,128)(2,1)S(1)} collective-permute-done((bf16[128,1024]{1,0:T(8,128)(2,1)S(1)}, bf16[128,1024]{1,0:T(8,128)(2,1)S(1)}, u32[]{:S(2)}, u32[]{:S(2)}) %collective-permute-start.18) | collective-permute-done | bytes 262176 | tf_op jit(solution)/shard_map/ppermute | solution.py:228
  82.1 8.3 %collective-permute-done.20.refs_1_ = bf16[128,1024]{1,0:T(8,128)(2,1)S(1)} collective-permute-done((bf16[128,1024]{1,0:T(8,128)(2,1)S(1)}, bf16[128,1024]{1,0:T(8,128)(2,1)S(1)}, u32[]{:S(2)}, u32[]{:S(2)}) %collective-permute-start.20) | collective-permute-done | bytes 262176 | tf_op jit(solution)/shard_map/ppermute | solution.py:228
  91.9 13.6 %collective-permute-done.23.refs_0_ = bf16[128,1024]{1,0:T(8,128)(2,1)S(1)} collective-permute-done((bf16[128,1024]{1,0:T(8,128)(2,1)}, bf16[128,1024]{1,0:T(8,128)(2,1)S(1)}, u32[]{:S(2)}, u32[]{:S(2)}) %collective-permute-start.23) | collective-permute-done | bytes 262176 | tf_op jit(solution)/shard_map/ppermute | solution.py:228
  107.9 4.4 %normalizers.2.refs_3_ = f32[8,512]{1,0:T(8,128)S(1)} custom-call(bf16[128,1024]{1,0:T(8,128)(2,1)S(1)} %copy-done, bf16[128,1024]{1,0:T(8,128)(2,1)S(1)} %collective-permute-done.25.refs_1_, f32[1,256]{1,0:T(1,128)S(1)} %bitcast.15, bf16[256,1024]{1,0:T(8,128)(2,1)S(1)} %get-tuple-element.14.a_ref.refs_0_.refs_3_.refs_4_, ...), custom_call_target="tpu_custom_call" | custom-call | flops 2147483648 | bytes 8912896 | tf_op jit(solution)/shard_map/normalizers/pallas_call | solution.py:206
  113.6 4.4 %normalizers.3 = f32[8,512]{1,0:T(8,128)S(1)} custom-call(bf16[128,1024]{1,0:T(8,128)(2,1)S(1)} %collective-permute-done.23.refs_0_, bf16[128,1024]{1,0:T(8,128)(2,1)S(1)} %collective-permute-done.24.refs_1_, f32[1,256]{1,0:T(1,128)S(1)} %bitcast.14, f32[8,512]{1,0:T(8,128)S(1)} %normalizers.2.refs_3_, ...), custom_call_target="tpu_custom_call" | custom-call | flops 2147483648 | bytes 8912896 | tf_op jit(solution)/shard_map/normalizers/pallas_call | solution.py:206
  118.1 3.6 %collective-permute-done.26 = f32[4,512]{1,0:T(4,128)S(1)} collective-permute-done((f32[4,512]{1,0:T(4,128)S(1)}, f32[4,512]{1,0:T(4,128)S(1)}, u32[]{:S(2)}, u32[]{:S(2)}) %collective-permute-start.26) | collective-permute-done | bytes 8224 | tf_op jit(solution)/shard_map/ppermute | solution.py:228
  122.1 3.4 %collective-permute-done.27 = f32[2,512]{1,0:T(2,128)S(1)} collective-permute-done((f32[2,512]{1,0:T(2,128)S(1)}, f32[2,512]{1,0:T(2,128)S(1)}, u32[]{:S(2)}, u32[]{:S(2)}) %collective-permute-start.27) | collective-permute-done | bytes 4128 | tf_op jit(solution)/shard_map/ppermute | solution.py:228
  (73 shorter events, 22.4 us)
Async XLA Ops:
  2.2 26.5 %collective-permute-start.17 = (bf16[256,1024]{1,0:T(8,128)(2,1)S(1)}, bf16[256,1024]{1,0:T(8,128)(2,1)S(1)}, u32[]{:S(2)}, u32[]{:S(2)}) collective-permute-start(bf16[256,1024]{1,0:T(8,128)(2,1)S(1)} %get-tuple-element.15.b_ref.refs_1_.refs_4_.refs_5_), channel_id=1, source_target_pairs={{0,1},{1,0},{2,3},{3,2},{4,5},{5,4},{6,7},{7,6},{8,9},{9,8},{10,11... | collective-permute-start | bytes 1572872 | tf_op jit(solution)/shard_map/ppermute | solution.py:228
  2.7 24.1 %collective-permute-start.5 = (bf16[256,1024]{1,0:T(8,128)(2,1)S(1)}, bf16[256,1024]{1,0:T(8,128)(2,1)S(1)}, u32[]{:S(2)}, u32[]{:S(2)}) collective-permute-start(bf16[256,1024]{1,0:T(8,128)(2,1)S(1)} %get-tuple-element.15.b_ref.refs_1_.refs_4_.refs_5_), channel_id=1, source_target_pairs={{0,2},{1,3},{2,0},{3,1},{4,6},{5,7},{6,4},{7,5},{8,10},{9,11},{10,... | collective-permute-start | bytes 1572872 | tf_op jit(solution)/shard_map/ppermute | solution.py:228
  5.3 21.4 %collective-permute-start.16 = (bf16[256,1024]{1,0:T(8,128)(2,1)S(1)}, bf16[256,1024]{1,0:T(8,128)(2,1)S(1)}, u32[]{:S(2)}, u32[]{:S(2)}) collective-permute-start(bf16[256,1024]{1,0:T(8,128)(2,1)S(1)} %get-tuple-element.14.a_ref.refs_0_.refs_3_.refs_4_), channel_id=1, source_target_pairs={{0,1},{1,0},{2,3},{3,2},{4,5},{5,4},{6,7},{7,6},{8,9},{9,8},{10,11... | collective-permute-start | bytes 1572872 | tf_op jit(solution)/shard_map/ppermute | solution.py:228
  5.4 21.4 %collective-permute-start.3 = (bf16[256,1024]{1,0:T(8,128)(2,1)S(1)}, bf16[256,1024]{1,0:T(8,128)(2,1)S(1)}, u32[]{:S(2)}, u32[]{:S(2)}) collective-permute-start(bf16[256,1024]{1,0:T(8,128)(2,1)S(1)} %get-tuple-element.14.a_ref.refs_0_.refs_3_.refs_4_), channel_id=1, source_target_pairs={{0,8},{1,9},{2,10},{3,11},{4,12},{5,13},{6,14},{7,15},{8,0},{9,1},... | collective-permute-start | bytes 1572872 | tf_op jit(solution)/shard_map/ppermute | solution.py:228
  26.1 15.0 %collective-permute-start.13 = (bf16[256,1024]{1,0:T(8,128)(2,1)S(1)}, bf16[256,1024]{1,0:T(8,128)(2,1)}, u32[]{:S(2)}, u32[]{:S(2)}) collective-permute-start(bf16[256,1024]{1,0:T(8,128)(2,1)S(1)} %get-tuple-element.14.a_ref.refs_0_.refs_3_.refs_4_), channel_id=1, source_target_pairs={{0,2},{1,3},{2,0},{3,1},{4,6},{5,7},{6,4},{7,5},{8,10},{9,11},{10,... | collective-permute-start | bytes 1572872 | tf_op jit(solution)/shard_map/ppermute | solution.py:228
  26.6 15.0 %collective-permute-start.9 = (bf16[256,1024]{1,0:T(8,128)(2,1)S(1)}, bf16[256,1024]{1,0:T(8,128)(2,1)}, u32[]{:S(2)}, u32[]{:S(2)}) collective-permute-start(bf16[256,1024]{1,0:T(8,128)(2,1)S(1)} %get-tuple-element.15.b_ref.refs_1_.refs_4_.refs_5_), channel_id=1, source_target_pairs={{0,8},{1,9},{2,10},{3,11},{4,12},{5,13},{6,14},{7,15},{8,0},{9,1},... | collective-permute-start | bytes 1572872 | tf_op jit(solution)/shard_map/ppermute | solution.py:228
  26.8 14.9 %collective-permute-start.15 = (bf16[256,1024]{1,0:T(8,128)(2,1)S(1)}, bf16[256,1024]{1,0:T(8,128)(2,1)}, u32[]{:S(2)}, u32[]{:S(2)}) collective-permute-start(bf16[256,1024]{1,0:T(8,128)(2,1)S(1)} %collective-permute-done.5.refs_1_.refs_8_.refs_9_), channel_id=1, source_target_pairs={{0,1},{1,0},{2,3},{3,2},{4,5},{5,4},{6,7},{7,6},{8,9},{9,8},{10,11... | collective-permute-start | bytes 1572872 | tf_op jit(solution)/shard_map/ppermute | solution.py:228
  26.8 22.3 %collective-permute-start.4 = (bf16[256,1024]{1,0:T(8,128)(2,1)S(1)}, bf16[256,1024]{1,0:T(8,128)(2,1)}, u32[]{:S(2)}, u32[]{:S(2)}) collective-permute-start(bf16[256,1024]{1,0:T(8,128)(2,1)S(1)} %collective-permute-done.3.refs_0_.refs_11_.refs_12_), channel_id=1, source_target_pairs={{0,2},{1,3},{2,0},{3,1},{4,6},{5,7},{6,4},{7,5},{8,10},{9,11},{10,... | collective-permute-start | bytes 1572872 | tf_op jit(solution)/shard_map/ppermute | solution.py:228
  28.6 20.7 %collective-permute-start.6 = (bf16[256,1024]{1,0:T(8,128)(2,1)S(1)}, bf16[256,1024]{1,0:T(8,128)(2,1)}, u32[]{:S(2)}, u32[]{:S(2)}) collective-permute-start(bf16[256,1024]{1,0:T(8,128)(2,1)S(1)} %collective-permute-done.5.refs_1_.refs_8_.refs_9_), channel_id=1, source_target_pairs={{0,8},{1,9},{2,10},{3,11},{4,12},{5,13},{6,14},{7,15},{8,0},{9,1},... | collective-permute-start | bytes 1572872 | tf_op jit(solution)/shard_map/ppermute | solution.py:228
  41.1 11.5 %collective-permute-start.14 = (bf16[256,1024]{1,0:T(8,128)(2,1)}, bf16[256,1024]{1,0:T(8,128)(2,1)S(1)}, u32[]{:S(2)}, u32[]{:S(2)}) collective-permute-start(bf16[256,1024]{1,0:T(8,128)(2,1)} %collective-permute-done.13.refs_0_.refs_7_.refs_8_), channel_id=1, source_target_pairs={{0,1},{1,0},{2,3},{3,2},{4,5},{5,4},{6,7},{7,6},{8,9},{9,8},{10,11... | collective-permute-start | bytes 1572872 | tf_op jit(solution)/shard_map/ppermute | solution.py:228
  41.6 16.6 %collective-permute-start.10 = (bf16[256,1024]{1,0:T(8,128)(2,1)S(1)}, bf16[256,1024]{1,0:T(8,128)(2,1)S(1)}, u32[]{:S(2)}, u32[]{:S(2)}) collective-permute-start(bf16[256,1024]{1,0:T(8,128)(2,1)S(1)} %collective-permute-done.3.refs_0_.refs_11_.refs_12_), channel_id=1, source_target_pairs={{0,1},{1,0},{2,3},{3,2},{4,5},{5,4},{6,7},{7,6},{8,9},{9,8},{10,11... | collective-permute-start | bytes 1572872 | tf_op jit(solution)/shard_map/ppermute | solution.py:228
  41.7 16.4 %collective-permute-start.11 = (bf16[256,1024]{1,0:T(8,128)(2,1)}, bf16[256,1024]{1,0:T(8,128)(2,1)S(1)}, u32[]{:S(2)}, u32[]{:S(2)}) collective-permute-start(bf16[256,1024]{1,0:T(8,128)(2,1)} %collective-permute-done.9.refs_1_.refs_12_.refs_13_), channel_id=1, source_target_pairs={{0,1},{1,0},{2,3},{3,2},{4,5},{5,4},{6,7},{7,6},{8,9},{9,8},{10,11... | collective-permute-start | bytes 1572872 | tf_op jit(solution)/shard_map/ppermute | solution.py:228
  49.1 13.2 %collective-permute-start.7 = (bf16[256,1024]{1,0:T(8,128)(2,1)}, bf16[256,1024]{1,0:T(8,128)(2,1)S(1)}, u32[]{:S(2)}, u32[]{:S(2)}) collective-permute-start(bf16[256,1024]{1,0:T(8,128)(2,1)} %collective-permute-done.4.refs_0_.refs_15_.refs_16_), channel_id=1, source_target_pairs={{0,1},{1,0},{2,3},{3,2},{4,5},{5,4},{6,7},{7,6},{8,9},{9,8},{10,11... | collective-permute-start | bytes 1572872 | tf_op jit(solution)/shard_map/ppermute | solution.py:228
  49.3 13.0 %collective-permute-start.8 = (bf16[256,1024]{1,0:T(8,128)(2,1)}, bf16[256,1024]{1,0:T(8,128)(2,1)S(1)}, u32[]{:S(2)}, u32[]{:S(2)}) collective-permute-start(bf16[256,1024]{1,0:T(8,128)(2,1)} %collective-permute-done.6.refs_1_.refs_16_.refs_17_), channel_id=1, source_target_pairs={{0,1},{1,0},{2,3},{3,2},{4,5},{5,4},{6,7},{7,6},{8,9},{9,8},{10,11... | collective-permute-start | bytes 1572872 | tf_op jit(solution)/shard_map/ppermute | solution.py:228
  52.6 9.7 %collective-permute-start.2 = (f32[2,512]{1,0:T(2,128)S(1)}, f32[2,512]{1,0:T(2,128)S(1)}, u32[]{:S(2)}, u32[]{:S(2)}) collective-permute-start(f32[2,512]{1,0:T(2,128)S(1)} %collective-permute-done.1.inv_ref), channel_id=1, source_target_pairs={{0,2},{1,3},{2,0},{3,1},{4,6},{5,7},{6,4},{7,5},{8,10},{9,11},{10,... | collective-permute-start | bytes 12296 | tf_op jit(solution)/shard_map/ppermute | solution.py:228
  66.5 3.9 %collective-permute-start.21 = (f32[4,128]{1,0:T(4,128)S(1)}, f32[4,128]{1,0:T(4,128)S(1)}, u32[]{:S(2)}, u32[]{:S(2)}) collective-permute-start(f32[4,128]{1,0:T(4,128)S(1)} %bitcast.16), channel_id=1, source_target_pairs={{0,4},{1,5},{2,6},{3,7},{4,0},{5,1},{6,2},{7,3},{8,12},{9,13},{10,... | collective-permute-start | bytes 6152 | tf_op jit(solution)/shard_map/ppermute | solution.py:228
  68.1 9.4 %collective-permute-start.19 = (bf16[128,1024]{1,0:T(8,128)(2,1)S(1)}, bf16[128,1024]{1,0:T(8,128)(2,1)S(1)}, u32[]{:S(2)}, u32[]{:S(2)}) collective-permute-start(bf16[128,1024]{1,0:T(8,128)(2,1)S(1)} %get-tuple-element.31), channel_id=1, source_target_pairs={{0,4},{1,5},{2,6},{3,7},{4,0},{5,1},{6,2},{7,3},{8,12},{9,13},{10,... | collective-permute-start | bytes 786440 | tf_op jit(solution)/shard_map/ppermute | solution.py:228
  68.9 13.3 %collective-permute-start.18 = (bf16[128,1024]{1,0:T(8,128)(2,1)S(1)}, bf16[128,1024]{1,0:T(8,128)(2,1)S(1)}, u32[]{:S(2)}, u32[]{:S(2)}) collective-permute-start(bf16[128,1024]{1,0:T(8,128)(2,1)S(1)} %get-tuple-element.32), channel_id=1, source_target_pairs={{0,4},{1,5},{2,6},{3,7},{4,0},{5,1},{6,2},{7,3},{8,12},{9,13},{10,... | collective-permute-start | bytes 786440 | tf_op jit(solution)/shard_map/ppermute | solution.py:228
  70.4 9.9 %collective-permute-start.22 = (f32[4,128]{1,0:T(4,128)S(1)}, f32[4,128]{1,0:T(4,128)S(1)}, u32[]{:S(2)}, u32[]{:S(2)}) collective-permute-start(f32[4,128]{1,0:T(4,128)S(1)} %maximum_add_fusion), channel_id=1, source_target_pairs={{0,16},{1,17},{2,18},{3,19},{4,20},{5,21},{6,22},{7,23},{8,24},{9,... | collective-permute-start | bytes 6152 | tf_op jit(solution)/shard_map/ppermute | solution.py:228
  77.7 12.7 %collective-permute-start.20 = (bf16[128,1024]{1,0:T(8,128)(2,1)S(1)}, bf16[128,1024]{1,0:T(8,128)(2,1)S(1)}, u32[]{:S(2)}, u32[]{:S(2)}) collective-permute-start(bf16[128,1024]{1,0:T(8,128)(2,1)S(1)} %get-tuple-element.29), channel_id=1, source_target_pairs={{0,16},{1,17},{2,18},{3,19},{4,20},{5,21},{6,22},{7,23},{8,24},{9,... | collective-permute-start | bytes 786440 | tf_op jit(solution)/shard_map/ppermute | solution.py:228
  91.3 15.6 %collective-permute-start.25 = (bf16[128,1024]{1,0:T(8,128)(2,1)}, bf16[128,1024]{1,0:T(8,128)(2,1)S(1)}, u32[]{:S(2)}, u32[]{:S(2)}) collective-permute-start(bf16[128,1024]{1,0:T(8,128)(2,1)} %directions.1.refs_0_), channel_id=1, source_target_pairs={{0,4},{1,5},{2,6},{3,7},{4,0},{5,1},{6,2},{7,3},{8,12},{9,13},{10,... | collective-permute-start | bytes 786440 | tf_op jit(solution)/shard_map/ppermute | solution.py:228
  91.8 13.6 %collective-permute-start.23 = (bf16[128,1024]{1,0:T(8,128)(2,1)}, bf16[128,1024]{1,0:T(8,128)(2,1)S(1)}, u32[]{:S(2)}, u32[]{:S(2)}) collective-permute-start(bf16[128,1024]{1,0:T(8,128)(2,1)} %directions.1.refs_0_), channel_id=1, source_target_pairs={{0,16},{1,17},{2,18},{3,19},{4,20},{5,21},{6,22},{7,23},{8,24},{9,... | collective-permute-start | bytes 786440 | tf_op jit(solution)/shard_map/ppermute | solution.py:228
  105.4 8.2 %collective-permute-start.24 = (bf16[128,1024]{1,0:T(8,128)(2,1)S(1)}, bf16[128,1024]{1,0:T(8,128)(2,1)S(1)}, u32[]{:S(2)}, u32[]{:S(2)}) collective-permute-start(bf16[128,1024]{1,0:T(8,128)(2,1)S(1)} %collective-permute-done.23.refs_0_), channel_id=1, source_target_pairs={{0,4},{1,5},{2,6},{3,7},{4,0},{5,1},{6,2},{7,3},{8,12},{9,13},{10,... | collective-permute-start | bytes 786440 | tf_op jit(solution)/shard_map/ppermute | solution.py:228
  118.1 3.7 %collective-permute-start.26 = (f32[4,512]{1,0:T(4,128)S(1)}, f32[4,512]{1,0:T(4,128)S(1)}, u32[]{:S(2)}, u32[]{:S(2)}) collective-permute-start(f32[4,512]{1,0:T(4,128)S(1)} %slice.86), channel_id=1, source_target_pairs={{0,8},{1,9},{2,10},{3,11},{4,12},{5,13},{6,14},{7,15},{8,0},{9,1},... | collective-permute-start | bytes 24584 | tf_op jit(solution)/shard_map/ppermute | solution.py:228
  (10 other events, 40.1 us)

commit v2 on v1

v2 whole, which is shorter than its diff:
```python
import functools

import jax
import jax.numpy as jnp
from jax import lax
from jax.experimental import pallas as pl
from jax.experimental.pallas import tpu as pltpu
from jax.sharding import PartitionSpec as P

KAPPA = 32
EPS = 1e-06
LANES = 128
ACROSS, ALONG = 1, 3
TAIL = 16
PARTS = 1
DENOM_MIB = 40
HASTE = 1
MIB = 1 << 20
F32, BF16 = jnp.float32, jnp.bfloat16
VMEM = pl.BlockSpec(memory_space=pltpu.VMEM)


def params(mib):
    return pltpu.CompilerParams(vmem_limit_bytes=mib * MIB)


def cost(macs, nbytes, exps=0):
    flops = 2 * macs // HASTE
    return pl.CostEstimate(flops=flops, bytes_accessed=nbytes // HASTE, transcendentals=exps // HASTE)


def column(row):
    return jnp.broadcast_to(row, (LANES, row.shape[1])).T


def nt_dot(a, b):
    return lax.dot_general(a, b, (((1,), (1,)), ((), ())), preferred_element_type=F32)


def exp_scores(comps, rows, shift):
    dots = nt_dot(comps, rows)
    return [
        jnp.exp(KAPPA * dots[:, j : j + LANES] + shift) for j in range(0, dots.shape[1], LANES)
    ]


def unit_kernel(e_ref, a_ref, b_ref):
    half = a_ref.shape[0]
    for i, out in enumerate((a_ref, b_ref)):
        x = e_ref[i * half : (i + 1) * half, :].astype(F32)
        out[...] = (x * lax.rsqrt(jnp.sum(x * x, 1, keepdims=True) + EPS)).astype(BF16)


def unit(emb):
    rows, dim = emb.shape
    half = jax.ShapeDtypeStruct((rows // 2, dim), BF16)
    return pl.pallas_call(
        unit_kernel,
        out_shape=(half, half),
        in_specs=[VMEM],
        out_specs=(VMEM, VMEM),
        compiler_params=params(24),
        cost_estimate=cost(0, 4 * rows * dim, rows),
        name="unit_rows",
    )(emb)


def gather(n, offsets, block, c_hbm, lw_ref, cen_out, lw_out, sems):
    me = lax.rem(lax.axis_index("rows"), n)
    copies = []
    for q, o in enumerate(offsets):
        owner = me ^ o
        source = c_hbm.at[pl.ds(pl.multiple_of(owner * block, block), block), :]
        copy = pltpu.make_async_copy(source, cen_out.at[q * block : (q + 1) * block, :], sems.at[q])
        copy.start()
        copies.append(copy)
        lw_out[q] = lw_ref[owner]
    return copies


def denom_kernel(n, offsets, c_ref, lw_ref, c_hbm, lws_ref, a_ref, b_ref, *refs):
    out_a, out_b, cen_out, lw_out, total, sems = refs
    block = cen_out.shape[0] // len(offsets)

    @pl.when(pl.program_id(0) == 0)
    def _():
        total[...] = jnp.zeros_like(total)
        for copy in gather(n, offsets, block, c_hbm, lws_ref, cen_out, lw_out, sems):
            copy.wait()

    shift = column(lw_ref[0])
    half = a_ref.shape[0]
    for i, rows in enumerate((a_ref, b_ref)):
        pieces = exp_scores(c_ref[...], rows[...], shift)
        total[:, i * half : (i + 1) * half] += jnp.concatenate(
            [jnp.sum(p, 0, keepdims=True) for p in pieces], 1
        )

    @pl.when(pl.program_id(0) == pl.num_programs(0) - 1)
    def _():
        weight = 1.0 / total[...]
        high = weight.astype(BF16).astype(F32)
        tail = jnp.concatenate([high, weight - high], 1)
        tail = jnp.broadcast_to(tail, (TAIL, tail.shape[1])).astype(BF16)
        for rows, out in ((a_ref, out_a), (b_ref, out_b)):
            out[:half, :] = rows[...]
            out[half:, : tail.shape[1]] = tail


def denominators(cen, lw, ua, ub, n, offsets):
    comps, dim = cen.shape
    half, block = ua.shape[0], comps // n
    tile = min(512, comps)
    whole = lambda shape: pl.BlockSpec(shape, lambda i: (0,) * len(shape))
    longer = jax.ShapeDtypeStruct((half + TAIL, dim), BF16)
    out_shape = (
        longer,
        longer,
        jax.ShapeDtypeStruct((len(offsets) * block, dim), BF16),
        jax.ShapeDtypeStruct((len(offsets), 1, block), F32),
    )
    return pl.pallas_call(
        functools.partial(denom_kernel, n, offsets),
        grid=(comps // tile,),
        out_shape=out_shape,
        in_specs=[
            pl.BlockSpec((tile, dim), lambda i: (i, 0)),
            pl.BlockSpec((1, 1, tile), lambda i: (i, 0, 0)),
            pl.BlockSpec(memory_space=pl.ANY),
            whole((n, 1, block)),
            whole((half, dim)),
            whole((half, dim)),
        ],
        out_specs=tuple(whole(o.shape) for o in out_shape),
        scratch_shapes=[
            pltpu.VMEM((1, 2 * half), F32),
            pltpu.SemaphoreType.DMA((len(offsets),)),
        ],
        compiler_params=params(DENOM_MIB),
        cost_estimate=cost(2 * half * comps * dim, 2 * (comps + 2 * half) * dim, 2 * half * comps),
        name="denominators",
    )(cen, lw.reshape(comps // tile, 1, tile), cen, lw.reshape(n, 1, block), ua, ub)


def sums_kernel(first, last, half, at, c_ref, lw_ref, tail_ref, *refs):
    pieces, refs = refs[:2], refs[2:]
    if not first:
        acc_in, cnt_in, refs = refs[0], refs[1], refs[2:]
    *outs, cnt_out = refs
    block = c_ref.shape[0] // lw_ref.shape[0]
    comps = slice(at, at + sum(out.shape[0] for out in outs))
    shift = jnp.concatenate(
        [column(lw_ref[q]) for q in range(comps.start // block, comps.stop // block)], 0
    )
    c = c_ref[comps, :]
    rows = 2 * half
    end = tail_ref.shape[0]
    tail = tail_ref[end - TAIL : end, : 2 * rows].astype(F32)[:1]
    weight = tail[:, :rows] + tail[:, rows:]
    count, total = None, None
    for i, piece in enumerate(pieces):
        u = piece[:half, :]
        resp = []
        for j, e in enumerate(exp_scores(c, u, shift)):
            lanes = i * half + j * LANES
            r = (e * weight[:, lanes : lanes + LANES]).astype(BF16)
            count = r.astype(F32) if count is None else count + r.astype(F32)
            resp.append(r)
        part = jnp.dot(jnp.concatenate(resp, 1), u, preferred_element_type=F32)
        total = part if total is None else total + part
    if not first:
        total = total + acc_in[comps, :]
        count = count + cnt_in[comps, :]
    start = 0
    for out in outs:
        out[...] = total[start : start + out.shape[0], :]
        start += out.shape[0]
    if last:
        for q in range(cnt_out.shape[0]):
            one = count[q * block : (q + 1) * block, :]
            cnt_out[q : q + 1, :] = jnp.sum(one.T, 0, keepdims=True)
    else:
        cnt_out[...] = count


def sums(cen, lw, tail, pieces, half, state, segment=None):
    comps, dim = cen.shape
    last = segment is not None
    first = state is None
    if last:
        at, size = segment
        block = lw.shape[2]
        out_shape = (jax.ShapeDtypeStruct((size // 2, dim), F32),) * 2
        out_shape += (jax.ShapeDtypeStruct((size // block, block), F32),)
    else:
        at, size = 0, comps
        out_shape = (
            jax.ShapeDtypeStruct((comps, dim), F32),
            jax.ShapeDtypeStruct((comps, LANES), F32),
        )
    args = [cen, lw, tail, *pieces] + ([] if first else list(state))
    aliases = {} if first or last else {len(args) - 2: 0, len(args) - 1: 1}
    return pl.pallas_call(
        functools.partial(sums_kernel, first, last, half, at),
        out_shape=out_shape,
        in_specs=[VMEM] * len(args),
        out_specs=(VMEM,) * len(out_shape),
        input_output_aliases=aliases,
        compiler_params=params(24),
        cost_estimate=cost(4 * half * size * dim, 2 * (size + 2 * half) * dim, 2 * half * size),
        name="sums",
    )(*args)


def merge_kernel(terms, finish, n_in, *refs):
    arrays, outs = refs[:n_in], refs[n_in:]
    for out, parts in zip(outs, terms):
        total = sum(arrays[i][at : at + out.shape[0], :].astype(F32) for i, at in parts)
        out[...] = finish(total).astype(out.dtype)


def normalize(x):
    return x * lax.rsqrt(jnp.sum(x * x, 1, keepdims=True) + EPS)


def merge(wanted, size, finish, name):
    arrays, terms = [], []
    for parts in wanted:
        term = []
        for x, at in parts:
            if not any(x is y for y in arrays):
                arrays.append(x)
            term.append((next(i for i, y in enumerate(arrays) if y is x), at))
        terms.append(term)
    dim = arrays[0].shape[1]
    out = jax.ShapeDtypeStruct((size, dim), BF16)
    return pl.pallas_call(
        functools.partial(merge_kernel, terms, finish, len(arrays)),
        out_shape=(out,) * len(wanted),
        in_specs=[VMEM] * len(arrays),
        out_specs=(VMEM,) * len(wanted),
        compiler_params=params(16),
        cost_estimate=cost(0, 12 * size * dim * len(wanted), size),
        name=name,
    )(*arrays)


def normalizer_kernel(n_comps, lw_rows, n_rows, half, *refs):
    comps, refs = refs[:n_comps], refs[n_comps:]
    lw_ref, refs = refs[0], refs[1:]
    pieces, refs = refs[: 2 * n_rows], refs[2 * n_rows :]
    before, outs = refs[:-n_rows], refs[-n_rows:]
    c = jnp.concatenate([r[...] for r in comps], 0)
    shift = jnp.concatenate([column(lw_ref[q : q + 1, :]) for q in lw_rows], 0)
    for i, out in enumerate(outs):
        for k in range(2):
            s = jnp.concatenate(
                [
                    jnp.sum(p, 0, keepdims=True)
                    for p in exp_scores(c, pieces[2 * i + k][:half, :], shift)
                ],
                1,
            )
            at = slice(None), slice(k * half, (k + 1) * half)
            out[at] = before[i][at] + s if before else s


def normalizers(comps, lw, lw_rows, before, pieces, half):
    dim = pieces[0].shape[1]
    n_comps, n_rows = sum(c.shape[0] for c in comps), len(pieces) // 2
    args = [*comps, lw, *pieces, *before]
    rows = 2 * half * n_rows
    return pl.pallas_call(
        functools.partial(normalizer_kernel, len(comps), lw_rows, n_rows, half),
        out_shape=(jax.ShapeDtypeStruct((1, 2 * half), F32),) * n_rows,
        in_specs=[VMEM] * len(args),
        out_specs=(VMEM,) * n_rows,
        compiler_params=params(24),
        cost_estimate=cost(rows * n_comps * dim, 2 * (n_comps + rows) * dim, rows * n_comps),
        name="normalizers",
    )(*args)


def local(embeddings, centroids, log_weights):
    n = lax.axis_size("rows")
    comps, dim = centroids.shape
    block = comps // n
    half = embeddings.shape[0] // 2
    row_total = embeddings.shape[0] * n
    me = lax.axis_index("rows")
    across, along = 1 << ACROSS, 1 << ALONG
    far = [1 << b for b in range(n.bit_length() - 1) if b not in (ACROSS, ALONG)]

    def swap(x, mask):
        return lax.ppermute(x, "rows", [(i, i ^ mask) for i in range(n)])

    offsets = [0]
    for mask in far:
        offsets = [o | m for o in offsets for m in (0, mask)]
    where = {o: q for q, o in enumerate(offsets)}

    ua, ub = unit(embeddings)
    xb, za = swap(ub, across), swap(ua, along)
    va, vb, cen, lw = denominators(centroids, log_weights, ua, ub, n, offsets)
    xa, zb = swap(va, across), swap(vb, along)
    da, db = swap(za, across), swap(xb, along)
    d_tail = swap(zb[half:], across)

    state = sums(cen, lw, va, (va, vb), half, None)
    state = sums(cen, lw, xa, (xa, xb), half, state)
    state = sums(cen, lw, zb, (za, zb), half, state)
    size = len(offsets) // 2 * block
    send0, send1, send_counts = sums(cen, lw, d_tail, (da, db), half, state, (size, size))
    keep0, keep1, keep_counts = sums(cen, lw, d_tail, (da, db), half, state, (0, size))

    got1 = swap(send1, far[0])
    got0 = swap(send0, far[0])
    quarter = len(offsets) // 4
    sub = block // PARTS
    parts = {}
    for pair, first in (((keep0, got0), 0), ((keep1, got1), quarter)):
        for q in range(quarter):
            for h in range(PARTS):
                parts[offsets[first + q], h] = [(x, q * block + h * sub) for x in pair]
    for k, mask in list(enumerate(far))[1:]:
        leaving = [o for o in reversed(offsets) if (o, 0) in parts and o & mask]
        items = [(o, h) for o in leaving for h in range(PARTS)]
        for group in [items] if k == 1 else [[i] for i in items]:
            merged = merge([parts.pop(i) for i in group], sub, lambda x: x, "merge")
            for (o, h), x in zip(group, merged):
                parts[o ^ mask, h].append((swap(x, mask), 0))
    dirs = {}
    for h in range(PARTS):
        (dirs[0, h],) = merge([parts[0, h]], sub, normalize, "directions")
    own_dirs = jnp.concatenate([dirs[0, h] for h in range(PARTS)])

    counts = jnp.concatenate([keep_counts, send_counts])
    for mask in far:
        order = [where[o ^ mask] for o in offsets]
        got = swap(counts, mask)
        counts = counts + jnp.concatenate([got[q : q + 1] for q in order])
    new_lw = jnp.log(counts / row_total)
    own_lw = new_lw[0]

    for mask in reversed(far[2:]):
        for o, h in list(dirs):
            dirs[o | mask, h] = swap(dirs[o, h], mask)
    pieces = (va, vb, xa, xb, za, zb, da, db)
    total = ()

    def arrived(os):
        return [dirs[o, h] for o in os for h in range(PARTS)]

    def send_all(os, mask, after=None):
        for o in os:
            for h in range(PARTS):
                x = dirs[o, h]
                if after is not None:
                    x, _ = lax.optimization_barrier((x, after))
                    dirs[o, h] = x
                dirs[o | mask, h] = swap(x, mask)

    def use(o, total):
        now = [o, o | far[0]]
        return normalizers(arrived(now), new_lw, [where[o] for o in now], total, pieces, half)

    near, *outer = [o for o in offsets if not o & (far[0] | far[1])]
    send_all([near], far[1])
    send_all([near], far[0])
    total = use(near, total)
    send_all(outer, far[1], total[0])
    send_all([near | far[1]], far[0], dirs[outer[0], 0] if outer else None)
    send_all(outer, far[0])
    for o in [near | far[1], *outer]:
        total = use(o, total)
    last = [o | far[1] for o in outer]
    send_all(last, far[0], total[0])
    for o in last:
        total = use(o, total)

    own, x, z, d = total
    whole = own + swap(d, across | along) + swap(z, along) + swap(x, across)
    return own_dirs, own_lw, jnp.log(whole[0])


def solution(mesh):
    return jax.shard_map(
        local,
        mesh=mesh,
        in_specs=(P(("grp", "rows"), None), P(), P()),
        out_specs=(P(("grp", "rows"), None), P(("grp", "rows")), P(("grp", "rows"))),
        check_vma=False,
    )
```

time: 128 us -> 105 us (0.82)
  waiting for transfers between devices: 61.4 us -> 46 us
  Pallas kernels: 31.9 us -> 24.9 us
    ppermute x29 -> x25, waiting for transfers between devices: 61.4 us -> 46 us  [swap(): return lax.ppermute(x, 'rows', [(i, i ^ mask) for i in range(n)])]
    pallas_call x8 -> x13, Pallas kernels: 31.6 us -> 24.6 us  [the longest x5 10.8 us: sums(): pl.pallas_call(functools.partial(sums_kernel, first, last, half, at), out...]
    dynamic_slice x2 -> x0, local copies, waits for them, and re-layouts: 2.12 us -> none  [the longest x1 1.28 us: local(): lax.dynamic_slice_in_dim(centroids, s, block)]
    unnamed x10 -> x16, local copies, waits for them, and re-layouts: 6.26 us -> 8.38 us
    ppermute x29 -> x25, starting transfers between devices: 23.8 us -> 23.7 us  [swap(): return lax.ppermute(x, 'rows', [(i, i ^ mask) for i in range(n)])]
  transfers between devices with their start and end apart: 29 -> 25, of which waited for: 15 -> 12; matrix products, arithmetic and copies ran while one was open for 2% -> 1% of each run, Pallas kernels for 17% -> 21%
where the time goes in v2:
time: 105 us
  waiting for transfers between devices  46 us (44%)
  Pallas kernels  24.9 us (24%)
  starting transfers between devices  23.7 us (23%)
  local copies, waits for them, and re-layouts  8.94 us (9%)
    ppermute x25, waiting for transfers between devices, swap(): return lax.ppermute(x, 'rows', [(i, i ^ mask) for i in range(n)])  46 us
    ppermute x25, starting transfers between devices, swap(): return lax.ppermute(x, 'rows', [(i, i ^ mask) for i in range(n)])  23.7 us
    pallas_call x5, Pallas kernels, sums(): pl.pallas_call(functools.partial(sums_kernel, first, last, half, at), out...  10.8 us
    unnamed x16, local copies, waits for them, and re-layouts  8.38 us
    pallas_call x1, Pallas kernels, denominators(): pl.pallas_call(functools.partial(denom_kernel, n, offsets), grid=(comps /...  6.77 us
    pallas_call x4, Pallas kernels, normalizers(): pl.pallas_call(functools.partial(normalizer_kernel, len(comps), lw_rows,...  6.01 us
  transfers between devices with their start and end apart: 25, of which 12 were waited for; matrix products, arithmetic and copies ran while one was open for 1% of the time, Pallas kernels for 21%

profile of v2, /device:TPU:0, one launch (start us, length us, event | category | flops | bytes accessed | tf_op | source)
XLA Modules:
  0.0 105.0 jit_solution(7257108909445729834)
XLA Ops:
  2.2 3.0 %collective-permute-start.4 = (bf16[256,1024]{1,0:T(8,128)(2,1)S(1)}, bf16[256,1024]{1,0:T(8,128)(2,1)S(1)}, u32[]{:S(2)}, u32[]{:S(2)}) collective-permute-start(bf16[256,1024]{1,0:T(8,128)(2,1)S(1)} %get-tuple-element.43.b_ref), channel_id=1, source_target_pairs={{0,2},{1,3},{2,0},{3,1},{4,6},{5,7},{6,4},{7,5},{8,10},{9,11},{10,... | collective-permute-start | bytes 1572872 | tf_op jit(solution)/shard_map/ppermute | solution.py:295
  5.2 1.6 %collective-permute-start.2 = (bf16[256,1024]{1,0:T(8,128)(2,1)S(1)}, bf16[256,1024]{1,0:T(8,128)(2,1)S(1)}, u32[]{:S(2)}, u32[]{:S(2)}) collective-permute-start(bf16[256,1024]{1,0:T(8,128)(2,1)S(1)} %get-tuple-element.42.a_ref), channel_id=1, source_target_pairs={{0,8},{1,9},{2,10},{3,11},{4,12},{5,13},{6,14},{7,15},{8,0},{9,1},... | collective-permute-start | bytes 1572872 | tf_op jit(solution)/shard_map/ppermute | solution.py:295
  6.8 3.4 %copy-done = bf16[4096,1024]{1,0:T(8,128)(2,1)S(1)} copy-done((bf16[4096,1024]{1,0:T(8,128)(2,1)S(1)}, bf16[4096,1024]{1,0:T(8,128)(2,1)}, u32[]{:S(2)}) %copy-start) | copy-done | bytes 8388632
  10.9 6.8 %denominators.1 = (bf16[272,1024]{1,0:T(8,128)(2,1)S(1)}, bf16[272,1024]{1,0:T(8,128)(2,1)S(1)}, bf16[1024,1024]{1,0:T(8,128)(2,1)S(1)}, f32[8,1,128]{2,1,0:T(1,128)S(1)}) custom-call(bf16[4096,1024]{1,0:T(8,128)(2,1)S(1)} %copy-done, f32[8,1,512]{2,1,0:T(1,128)S(1)} %bitcast.5, bf16[4096,1024]{1,0:T(8,128)(2,1)S(1)} %copy-done, f32[32,1,128]{2,1,0:T(1,128)S(1)} %bitcast.6, ...), custom_call_target="tpu_custom_call" | custom-call | flops 4294967296 | bytes 9437184 | tf_op jit(solution)/shard_map/denominators/pallas_call | solution.py:122
  18.6 1.6 %collective-permute-start.3 = (bf16[256,1024]{1,0:T(8,128)(2,1)S(1)}, bf16[256,1024]{1,0:T(8,128)(2,1)S(1)}, u32[]{:S(2)}, u32[]{:S(2)}) collective-permute-start(bf16[256,1024]{1,0:T(8,128)(2,1)S(1)} %collective-permute-done.2.refs_0_.refs_7_), channel_id=1, source_target_pairs={{0,2},{1,3},{2,0},{3,1},{4,6},{5,7},{6,4},{7,5},{8,10},{9,11},{10,... | collective-permute-start | bytes 1572872 | tf_op jit(solution)/shard_map/ppermute | solution.py:295
  20.2 1.6 %collective-permute-start.5 = (bf16[256,1024]{1,0:T(8,128)(2,1)S(1)}, bf16[256,1024]{1,0:T(8,128)(2,1)S(1)}, u32[]{:S(2)}, u32[]{:S(2)}) collective-permute-start(bf16[256,1024]{1,0:T(8,128)(2,1)S(1)} %collective-permute-done.4.refs_1_.refs_6_), channel_id=1, source_target_pairs={{0,8},{1,9},{2,10},{3,11},{4,12},{5,13},{6,14},{7,15},{8,0},{9,1},... | collective-permute-start | bytes 1572872 | tf_op jit(solution)/shard_map/ppermute | solution.py:295
  21.8 2.5 %sums.5 = (f32[1024,1024]{1,0:T(8,128)S(1)}, f32[1024,128]{1,0:T(8,128)S(1)}) custom-call(bf16[1024,1024]{1,0:T(8,128)(2,1)S(1)} %get-tuple-element.44.c_ref, f32[8,1,128]{2,1,0:T(1,128)S(1)} %get-tuple-element.45.lw_ref, bf16[272,1024]{1,0:T(8,128)(2,1)S(1)} %get-tuple-element.47.tail_ref.refs_0_.refs_3_, ...), custom_call_target="tpu_custom_call" | custom-call | flops 2147483648 | bytes 3145728 | tf_op jit(solution)/shard_map/sums/pallas_call | solution.py:203
  24.3 9.0 %collective-permute-done.tail_ref.refs_1_.refs_8_ = bf16[272,1024]{1,0:T(8,128)(2,1)S(1)} collective-permute-done((bf16[272,1024]{1,0:T(8,128)(2,1)S(1)}, bf16[272,1024]{1,0:T(8,128)(2,1)S(1)}, u32[]{:S(2)}, u32[]{:S(2)}) %collective-permute-start) | collective-permute-done | bytes 557088 | tf_op jit(solution)/shard_map/ppermute | solution.py:295
  33.8 2.7 %sums.6 = (f32[1024,1024]{1,0:T(8,128)S(1)}, f32[1024,128]{1,0:T(8,128)S(1)}) custom-call(bf16[1024,1024]{1,0:T(8,128)(2,1)S(1)} %get-tuple-element.44.c_ref, f32[8,1,128]{2,1,0:T(1,128)S(1)} %get-tuple-element.45.lw_ref, bf16[272,1024]{1,0:T(8,128)(2,1)S(1)} %collective-permute-done.6.tail_ref.refs_0_.refs_5_, ...), custom_call_target="tpu_custom_call", output_to_operand_aliasing={{0}: (5, {}), {1}: (6, {})} | custom-call | flops 2147483648 | bytes 3145728 | tf_op jit(solution)/shard_map/sums/pallas_call | solution.py:203
  36.6 2.7 %sums.7 = (f32[1024,1024]{1,0:T(8,128)S(1)}, f32[1024,128]{1,0:T(8,128)S(1)}) custom-call(bf16[1024,1024]{1,0:T(8,128)(2,1)S(1)} %get-tuple-element.44.c_ref, f32[8,1,128]{2,1,0:T(1,128)S(1)} %get-tuple-element.45.lw_ref, bf16[272,1024]{1,0:T(8,128)(2,1)S(1)} %collective-permute-done.tail_ref.refs_1_.refs_8_, ...), custom_call_target="tpu_custom_call", output_to_operand_aliasing={{0}: (5, {}), {1}: (6, {})} | custom-call | flops 2147483648 | bytes 3145728 | tf_op jit(solution)/shard_map/sums/pallas_call | solution.py:203
  39.3 4.3 %collective-permute-done.1.tail_ref = bf16[16,1024]{1,0:T(8,128)(2,1)S(1)} collective-permute-done((bf16[16,1024]{1,0:T(8,128)(2,1)S(1)}, bf16[16,1024]{1,0:T(8,128)(2,1)S(1)}, u32[]{:S(2)}, u32[]{:S(2)}) %collective-permute-start.1) | collective-permute-done | bytes 32800 | tf_op jit(solution)/shard_map/ppermute | solution.py:295
  47.9 1.6 %collective-permute-start.10 = (bf16[128,1024]{1,0:T(8,128)(2,1)S(1)}, bf16[128,1024]{1,0:T(8,128)(2,1)S(1)}, u32[]{:S(2)}, u32[]{:S(2)}) collective-permute-start(bf16[128,1024]{1,0:T(8,128)(2,1)S(1)} %get-tuple-element.59), channel_id=1, source_target_pairs={{0,4},{1,5},{2,6},{3,7},{4,0},{5,1},{6,2},{7,3},{8,12},{9,13},{10,... | collective-permute-start | bytes 786440 | tf_op jit(solution)/shard_map/ppermute | solution.py:295
  51.6 5.5 %collective-permute-done.10.refs_2_ = bf16[128,1024]{1,0:T(8,128)(2,1)S(1)} collective-permute-done((bf16[128,1024]{1,0:T(8,128)(2,1)S(1)}, bf16[128,1024]{1,0:T(8,128)(2,1)S(1)}, u32[]{:S(2)}, u32[]{:S(2)}) %collective-permute-start.10) | collective-permute-done | bytes 262176 | tf_op jit(solution)/shard_map/ppermute | solution.py:295
  57.1 2.7 %collective-permute-start.11 = (bf16[128,1024]{1,0:T(8,128)(2,1)S(1)}, bf16[128,1024]{1,0:T(8,128)(2,1)S(1)}, u32[]{:S(2)}, u32[]{:S(2)}) collective-permute-start(bf16[128,1024]{1,0:T(8,128)(2,1)S(1)} %merge.3), channel_id=1, source_target_pairs={{0,16},{1,17},{2,18},{3,19},{4,20},{5,21},{6,22},{7,23},{8,24},{9,... | collective-permute-start | bytes 786440 | tf_op jit(solution)/shard_map/ppermute | solution.py:295
  60.2 1.8 %collective-permute-done.9.refs_2_ = bf16[128,1024]{1,0:T(8,128)(2,1)S(1)} collective-permute-done((bf16[128,1024]{1,0:T(8,128)(2,1)S(1)}, bf16[128,1024]{1,0:T(8,128)(2,1)S(1)}, u32[]{:S(2)}, u32[]{:S(2)}) %collective-permute-start.9) | collective-permute-done | bytes 262176 | tf_op jit(solution)/shard_map/ppermute | solution.py:295
  62.0 8.6 %collective-permute-done.11.refs_3_ = bf16[128,1024]{1,0:T(8,128)(2,1)S(1)} collective-permute-done((bf16[128,1024]{1,0:T(8,128)(2,1)S(1)}, bf16[128,1024]{1,0:T(8,128)(2,1)S(1)}, u32[]{:S(2)}, u32[]{:S(2)}) %collective-permute-start.11) | collective-permute-done | bytes 262176 | tf_op jit(solution)/shard_map/ppermute | solution.py:295
  71.6 1.6 %collective-permute-start.19 = (bf16[128,1024]{1,0:T(8,128)(2,1)}, bf16[128,1024]{1,0:T(8,128)(2,1)S(1)}, u32[]{:S(2)}, u32[]{:S(2)}) collective-permute-start(bf16[128,1024]{1,0:T(8,128)(2,1)} %directions.1.refs_0_), channel_id=1, source_target_pairs={{0,4},{1,5},{2,6},{3,7},{4,0},{5,1},{6,2},{7,3},{8,12},{9,13},{10,... | collective-permute-start | bytes 786440 | tf_op jit(solution)/shard_map/ppermute | solution.py:295
  76.3 1.6 %normalizers.4 = (f32[1,512]{1,0:T(1,128)S(1)}, f32[1,512]{1,0:T(1,128)S(1)}, f32[1,512]{1,0:T(1,128)S(1)}, f32[1,512]{1,0:T(1,128)S(1)}) custom-call(bf16[128,1024]{1,0:T(8,128)(2,1)S(1)} %copy-done.6, bf16[128,1024]{1,0:T(8,128)(2,1)S(1)} %collective-permute-done.16.refs_1_, f32[8,128]{1,0:T(8,128)S(1)} %multiply_log_fusion.refs_2_, ...), custom_call_target="tpu_custom_call" | custom-call | flops 1073741824 | bytes 4718592 | tf_op jit(solution)/shard_map/normalizers/pallas_call | solution.py:273
  77.9 9.1 %collective-permute-done.15.refs_0_ = bf16[128,1024]{1,0:T(8,128)(2,1)S(1)} collective-permute-done((bf16[128,1024]{1,0:T(8,128)(2,1)}, bf16[128,1024]{1,0:T(8,128)(2,1)S(1)}, u32[]{:S(2)}, u32[]{:S(2)}) %collective-permute-start.15) | collective-permute-done | bytes 262176 | tf_op jit(solution)/shard_map/ppermute | solution.py:295
  87.6 1.5 %collective-permute-start.17 = (bf16[128,1024]{1,0:T(8,128)(2,1)S(1)}, bf16[128,1024]{1,0:T(8,128)(2,1)S(1)}, u32[]{:S(2)}, u32[]{:S(2)}) collective-permute-start(bf16[128,1024]{1,0:T(8,128)(2,1)S(1)} %collective-permute-done.15.refs_0_), channel_id=1, source_target_pairs={{0,4},{1,5},{2,6},{3,7},{4,0},{5,1},{6,2},{7,3},{8,12},{9,13},{10,... | collective-permute-start | bytes 786440 | tf_op jit(solution)/shard_map/ppermute | solution.py:295
  92.0 3.7 %collective-permute-done.17.refs_0_ = bf16[128,1024]{1,0:T(8,128)(2,1)S(1)} collective-permute-done((bf16[128,1024]{1,0:T(8,128)(2,1)S(1)}, bf16[128,1024]{1,0:T(8,128)(2,1)S(1)}, u32[]{:S(2)}, u32[]{:S(2)}) %collective-permute-start.17) | collective-permute-done | bytes 262176 | tf_op jit(solution)/shard_map/ppermute | solution.py:295
  95.8 1.5 %collective-permute-done.21.refs_1_ = bf16[128,1024]{1,0:T(8,128)(2,1)S(1)} collective-permute-done((bf16[128,1024]{1,0:T(8,128)(2,1)S(1)}, bf16[128,1024]{1,0:T(8,128)(2,1)S(1)}, u32[]{:S(2)}, u32[]{:S(2)}) %collective-permute-start.21) | collective-permute-done | bytes 262176 | tf_op jit(solution)/shard_map/ppermute | solution.py:295
  98.9 1.9 %collective-permute-start.23 = (f32[1,512]{1,0:T(1,128)S(1)}, f32[1,512]{1,0:T(1,128)S(1)}, u32[]{:S(2)}, u32[]{:S(2)}) collective-permute-start(f32[1,512]{1,0:T(1,128)S(1)} %get-tuple-element.79), channel_id=1, source_target_pairs={{0,8},{1,9},{2,10},{3,11},{4,12},{5,13},{6,14},{7,15},{8,0},{9,1},... | collective-permute-start | bytes 6152 | tf_op jit(solution)/shard_map/ppermute | solution.py:295
  100.8 1.5 %collective-permute-start.24 = (f32[1,512]{1,0:T(1,128)S(1)}, f32[1,512]{1,0:T(1,128)S(1)}, u32[]{:S(2)}, u32[]{:S(2)}) collective-permute-start(f32[1,512]{1,0:T(1,128)S(1)} %get-tuple-element.80), channel_id=1, source_target_pairs={{0,2},{1,3},{2,0},{3,1},{4,6},{5,7},{6,4},{7,5},{8,10},{9,11},{10,... | collective-permute-start | bytes 6152 | tf_op jit(solution)/shard_map/ppermute | solution.py:295
  (67 shorter events, 22.2 us)
Async XLA Ops:
  2.2 18.0 %collective-permute-start.4 = (bf16[256,1024]{1,0:T(8,128)(2,1)S(1)}, bf16[256,1024]{1,0:T(8,128)(2,1)S(1)}, u32[]{:S(2)}, u32[]{:S(2)}) collective-permute-start(bf16[256,1024]{1,0:T(8,128)(2,1)S(1)} %get-tuple-element.43.b_ref), channel_id=1, source_target_pairs={{0,2},{1,3},{2,0},{3,1},{4,6},{5,7},{6,4},{7,5},{8,10},{9,11},{10,... | collective-permute-start | bytes 1572872 | tf_op jit(solution)/shard_map/ppermute | solution.py:295
  5.2 13.4 %collective-permute-start.2 = (bf16[256,1024]{1,0:T(8,128)(2,1)S(1)}, bf16[256,1024]{1,0:T(8,128)(2,1)S(1)}, u32[]{:S(2)}, u32[]{:S(2)}) collective-permute-start(bf16[256,1024]{1,0:T(8,128)(2,1)S(1)} %get-tuple-element.42.a_ref), channel_id=1, source_target_pairs={{0,8},{1,9},{2,10},{3,11},{4,12},{5,13},{6,14},{7,15},{8,0},{9,1},... | collective-permute-start | bytes 1572872 | tf_op jit(solution)/shard_map/ppermute | solution.py:295
  17.7 15.6 %collective-permute-start = (bf16[272,1024]{1,0:T(8,128)(2,1)S(1)}, bf16[272,1024]{1,0:T(8,128)(2,1)S(1)}, u32[]{:S(2)}, u32[]{:S(2)}) collective-permute-start(bf16[272,1024]{1,0:T(8,128)(2,1)S(1)} %get-tuple-element.46.refs_1_.refs_4_), channel_id=1, source_target_pairs={{0,8},{1,9},{2,10},{3,11},{4,12},{5,13},{6,14},{7,15},{8,0},{9,1},... | collective-permute-start | bytes 1671176 | tf_op jit(solution)/shard_map/ppermute | solution.py:295
  18.2 15.6 %collective-permute-start.6 = (bf16[272,1024]{1,0:T(8,128)(2,1)S(1)}, bf16[272,1024]{1,0:T(8,128)(2,1)S(1)}, u32[]{:S(2)}, u32[]{:S(2)}) collective-permute-start(bf16[272,1024]{1,0:T(8,128)(2,1)S(1)} %get-tuple-element.47.tail_ref.refs_0_.refs_3_), channel_id=1, source_target_pairs={{0,2},{1,3},{2,0},{3,1},{4,6},{5,7},{6,4},{7,5},{8,10},{9,11},{10,... | collective-permute-start | bytes 1671176 | tf_op jit(solution)/shard_map/ppermute | solution.py:295
  18.6 25.1 %collective-permute-start.3 = (bf16[256,1024]{1,0:T(8,128)(2,1)S(1)}, bf16[256,1024]{1,0:T(8,128)(2,1)S(1)}, u32[]{:S(2)}, u32[]{:S(2)}) collective-permute-start(bf16[256,1024]{1,0:T(8,128)(2,1)S(1)} %collective-permute-done.2.refs_0_.refs_7_), channel_id=1, source_target_pairs={{0,2},{1,3},{2,0},{3,1},{4,6},{5,7},{6,4},{7,5},{8,10},{9,11},{10,... | collective-permute-start | bytes 1572872 | tf_op jit(solution)/shard_map/ppermute | solution.py:295
  20.2 23.4 %collective-permute-start.5 = (bf16[256,1024]{1,0:T(8,128)(2,1)S(1)}, bf16[256,1024]{1,0:T(8,128)(2,1)S(1)}, u32[]{:S(2)}, u32[]{:S(2)}) collective-permute-start(bf16[256,1024]{1,0:T(8,128)(2,1)S(1)} %collective-permute-done.4.refs_1_.refs_6_), channel_id=1, source_target_pairs={{0,8},{1,9},{2,10},{3,11},{4,12},{5,13},{6,14},{7,15},{8,0},{9,1},... | collective-permute-start | bytes 1572872 | tf_op jit(solution)/shard_map/ppermute | solution.py:295
  33.3 10.3 %collective-permute-start.1 = (bf16[16,1024]{1,0:T(8,128)(2,1)S(1)}, bf16[16,1024]{1,0:T(8,128)(2,1)S(1)}, u32[]{:S(2)}, u32[]{:S(2)}) collective-permute-start(bf16[16,1024]{1,0:T(8,128)(2,1)S(1)} %slice.80), channel_id=1, source_target_pairs={{0,2},{1,3},{2,0},{3,1},{4,6},{5,7},{6,4},{7,5},{8,10},{9,11},{10,... | collective-permute-start | bytes 98312 | tf_op jit(solution)/shard_map/ppermute | solution.py:295
  45.0 2.7 %collective-permute-start.8 = (f32[256,1024]{1,0:T(8,128)S(1)}, f32[256,1024]{1,0:T(8,128)S(1)}, u32[]{:S(2)}, u32[]{:S(2)}) collective-permute-start(f32[256,1024]{1,0:T(8,128)S(1)} %get-tuple-element.57), channel_id=1, source_target_pairs={{0,1},{1,0},{2,3},{3,2},{4,5},{5,4},{6,7},{7,6},{8,9},{9,8},{10,11... | collective-permute-start | bytes 3145736 | tf_op jit(solution)/shard_map/ppermute | solution.py:295
  45.1 6.4 %collective-permute-start.7 = (f32[256,1024]{1,0:T(8,128)S(1)}, f32[256,1024]{1,0:T(8,128)S(1)}, u32[]{:S(2)}, u32[]{:S(2)}) collective-permute-start(f32[256,1024]{1,0:T(8,128)S(1)} %get-tuple-element.55), channel_id=1, source_target_pairs={{0,1},{1,0},{2,3},{3,2},{4,5},{5,4},{6,7},{7,6},{8,9},{9,8},{10,11... | collective-permute-start | bytes 3145736 | tf_op jit(solution)/shard_map/ppermute | solution.py:295
  47.0 2.4 %collective-permute-start.12 = (f32[8,128]{1,0:T(8,128)S(1)}, f32[8,128]{1,0:T(8,128)S(1)}, u32[]{:S(2)}, u32[]{:S(2)}) collective-permute-start(f32[8,128]{1,0:T(8,128)S(1)} %pad_maximum_fusion), channel_id=1, source_target_pairs={{0,1},{1,0},{2,3},{3,2},{4,5},{5,4},{6,7},{7,6},{8,9},{9,8},{10,11... | collective-permute-start | bytes 12296 | tf_op jit(solution)/shard_map/ppermute | solution.py:295
  47.9 9.2 %collective-permute-start.10 = (bf16[128,1024]{1,0:T(8,128)(2,1)S(1)}, bf16[128,1024]{1,0:T(8,128)(2,1)S(1)}, u32[]{:S(2)}, u32[]{:S(2)}) collective-permute-start(bf16[128,1024]{1,0:T(8,128)(2,1)S(1)} %get-tuple-element.59), channel_id=1, source_target_pairs={{0,4},{1,5},{2,6},{3,7},{4,0},{5,1},{6,2},{7,3},{8,12},{9,13},{10,... | collective-permute-start | bytes 786440 | tf_op jit(solution)/shard_map/ppermute | solution.py:295
  49.5 10.3 %collective-permute-start.13 = (f32[8,128]{1,0:T(8,128)S(1)}, f32[8,128]{1,0:T(8,128)S(1)}, u32[]{:S(2)}, u32[]{:S(2)}) collective-permute-start(f32[8,128]{1,0:T(8,128)S(1)} %maximum_add_fusion), channel_id=1, source_target_pairs={{0,4},{1,5},{2,6},{3,7},{4,0},{5,1},{6,2},{7,3},{8,12},{9,13},{10,... | collective-permute-start | bytes 12296 | tf_op jit(solution)/shard_map/ppermute | solution.py:295
  50.9 11.1 %collective-permute-start.9 = (bf16[128,1024]{1,0:T(8,128)(2,1)S(1)}, bf16[128,1024]{1,0:T(8,128)(2,1)S(1)}, u32[]{:S(2)}, u32[]{:S(2)}) collective-permute-start(bf16[128,1024]{1,0:T(8,128)(2,1)S(1)} %get-tuple-element.58), channel_id=1, source_target_pairs={{0,4},{1,5},{2,6},{3,7},{4,0},{5,1},{6,2},{7,3},{8,12},{9,13},{10,... | collective-permute-start | bytes 786440 | tf_op jit(solution)/shard_map/ppermute | solution.py:295
  57.1 13.4 %collective-permute-start.11 = (bf16[128,1024]{1,0:T(8,128)(2,1)S(1)}, bf16[128,1024]{1,0:T(8,128)(2,1)S(1)}, u32[]{:S(2)}, u32[]{:S(2)}) collective-permute-start(bf16[128,1024]{1,0:T(8,128)(2,1)S(1)} %merge.3), channel_id=1, source_target_pairs={{0,16},{1,17},{2,18},{3,19},{4,20},{5,21},{6,22},{7,23},{8,24},{9,... | collective-permute-start | bytes 786440 | tf_op jit(solution)/shard_map/ppermute | solution.py:295
  59.8 11.7 %collective-permute-start.14 = (f32[8,128]{1,0:T(8,128)S(1)}, f32[8,128]{1,0:T(8,128)S(1)}, u32[]{:S(2)}, u32[]{:S(2)}) collective-permute-start(f32[8,128]{1,0:T(8,128)S(1)} %maximum_add_fusion.1), channel_id=1, source_target_pairs={{0,16},{1,17},{2,18},{3,19},{4,20},{5,21},{6,22},{7,23},{8,24},{9,... | collective-permute-start | bytes 12296 | tf_op jit(solution)/shard_map/ppermute | solution.py:295
  71.5 1.7 %collective-permute-start.16 = (bf16[128,1024]{1,0:T(8,128)(2,1)}, bf16[128,1024]{1,0:T(8,128)(2,1)S(1)}, u32[]{:S(2)}, u32[]{:S(2)}) collective-permute-start(bf16[128,1024]{1,0:T(8,128)(2,1)} %directions.1.refs_0_), channel_id=1, source_target_pairs={{0,1},{1,0},{2,3},{3,2},{4,5},{5,4},{6,7},{7,6},{8,9},{9,8},{10,11... | collective-permute-start | bytes 786440 | tf_op jit(solution)/shard_map/ppermute | solution.py:295
  71.5 15.5 %collective-permute-start.15 = (bf16[128,1024]{1,0:T(8,128)(2,1)}, bf16[128,1024]{1,0:T(8,128)(2,1)S(1)}, u32[]{:S(2)}, u32[]{:S(2)}) collective-permute-start(bf16[128,1024]{1,0:T(8,128)(2,1)} %directions.1.refs_0_), channel_id=1, source_target_pairs={{0,16},{1,17},{2,18},{3,19},{4,20},{5,21},{6,22},{7,23},{8,24},{9,... | collective-permute-start | bytes 786440 | tf_op jit(solution)/shard_map/ppermute | solution.py:295
  71.6 15.4 %collective-permute-start.19 = (bf16[128,1024]{1,0:T(8,128)(2,1)}, bf16[128,1024]{1,0:T(8,128)(2,1)S(1)}, u32[]{:S(2)}, u32[]{:S(2)}) collective-permute-start(bf16[128,1024]{1,0:T(8,128)(2,1)} %directions.1.refs_0_), channel_id=1, source_target_pairs={{0,4},{1,5},{2,6},{3,7},{4,0},{5,1},{6,2},{7,3},{8,12},{9,13},{10,... | collective-permute-start | bytes 786440 | tf_op jit(solution)/shard_map/ppermute | solution.py:295
  87.0 2.0 %collective-permute-start.20 = (bf16[128,1024]{1,0:T(8,128)(2,1)S(1)}, bf16[128,1024]{1,0:T(8,128)(2,1)S(1)}, u32[]{:S(2)}, u32[]{:S(2)}) collective-permute-start(bf16[128,1024]{1,0:T(8,128)(2,1)S(1)} %collective-permute-done.19.refs_0_), channel_id=1, source_target_pairs={{0,1},{1,0},{2,3},{3,2},{4,5},{5,4},{6,7},{7,6},{8,9},{9,8},{10,11... | collective-permute-start | bytes 786440 | tf_op jit(solution)/shard_map/ppermute | solution.py:295
  87.0 3.5 %collective-permute-start.18 = (bf16[128,1024]{1,0:T(8,128)(2,1)S(1)}, bf16[128,1024]{1,0:T(8,128)(2,1)S(1)}, u32[]{:S(2)}, u32[]{:S(2)}) collective-permute-start(bf16[128,1024]{1,0:T(8,128)(2,1)S(1)} %collective-permute-done.15.refs_0_), channel_id=1, source_target_pairs={{0,1},{1,0},{2,3},{3,2},{4,5},{5,4},{6,7},{7,6},{8,9},{9,8},{10,11... | collective-permute-start | bytes 786440 | tf_op jit(solution)/shard_map/ppermute | solution.py:295
  87.6 8.2 %collective-permute-start.17 = (bf16[128,1024]{1,0:T(8,128)(2,1)S(1)}, bf16[128,1024]{1,0:T(8,128)(2,1)S(1)}, u32[]{:S(2)}, u32[]{:S(2)}) collective-permute-start(bf16[128,1024]{1,0:T(8,128)(2,1)S(1)} %collective-permute-done.15.refs_0_), channel_id=1, source_target_pairs={{0,4},{1,5},{2,6},{3,7},{4,0},{5,1},{6,2},{7,3},{8,12},{9,13},{10,... | collective-permute-start | bytes 786440 | tf_op jit(solution)/shard_map/ppermute | solution.py:295
  98.8 4.5 %collective-permute-start.22 = (f32[1,512]{1,0:T(1,128)S(1)}, f32[1,512]{1,0:T(1,128)S(1)}, u32[]{:S(2)}, u32[]{:S(2)}) collective-permute-start(f32[1,512]{1,0:T(1,128)S(1)} %get-tuple-element.78), channel_id=1, source_target_pairs={{0,10},{1,11},{2,8},{3,9},{4,14},{5,15},{6,12},{7,13},{8,2},{9,3},... | collective-permute-start | bytes 6152 | tf_op jit(solution)/shard_map/ppermute | solution.py:295
  98.9 4.5 %collective-permute-start.23 = (f32[1,512]{1,0:T(1,128)S(1)}, f32[1,512]{1,0:T(1,128)S(1)}, u32[]{:S(2)}, u32[]{:S(2)}) collective-permute-start(f32[1,512]{1,0:T(1,128)S(1)} %get-tuple-element.79), channel_id=1, source_target_pairs={{0,8},{1,9},{2,10},{3,11},{4,12},{5,13},{6,14},{7,15},{8,0},{9,1},... | collective-permute-start | bytes 6152 | tf_op jit(solution)/shard_map/ppermute | solution.py:295
  100.8 3.6 %collective-permute-start.24 = (f32[1,512]{1,0:T(1,128)S(1)}, f32[1,512]{1,0:T(1,128)S(1)}, u32[]{:S(2)}, u32[]{:S(2)}) collective-permute-start(f32[1,512]{1,0:T(1,128)S(1)} %get-tuple-element.80), channel_id=1, source_target_pairs={{0,2},{1,3},{2,0},{3,1},{4,6},{5,7},{6,4},{7,5},{8,10},{9,11},{10,... | collective-permute-start | bytes 6152 | tf_op jit(solution)/shard_map/ppermute | solution.py:295
  (9 other events, 47.8 us)

commit v3 on v2

--- a/solution.py
+++ b/solution.py
@@ -12,9 +12,7 @@
 LANES = 128
 ACROSS, ALONG = 1, 3
 TAIL = 16
-PARTS = 1
-DENOM_MIB = 40
-HASTE = 1
+PARTS = 2
 MIB = 1 << 20
 F32, BF16 = jnp.float32, jnp.bfloat16
 VMEM = pl.BlockSpec(memory_space=pltpu.VMEM)
@@ -25,8 +23,7 @@
 
 
 def cost(macs, nbytes, exps=0):
-    flops = 2 * macs // HASTE
-    return pl.CostEstimate(flops=flops, bytes_accessed=nbytes // HASTE, transcendentals=exps // HASTE)
+    return pl.CostEstimate(flops=2 * macs, bytes_accessed=nbytes, transcendentals=exps)
 
 
 def column(row):
@@ -65,16 +62,13 @@
     )(emb)
 
 
-def gather(n, offsets, block, c_hbm, lw_ref, cen_out, lw_out, sems):
+def gather(n, offsets, block, c_hbm, cen_out, sems):
     me = lax.rem(lax.axis_index("rows"), n)
     copies = []
     for q, o in enumerate(offsets):
-        owner = me ^ o
-        source = c_hbm.at[pl.ds(pl.multiple_of(owner * block, block), block), :]
-        copy = pltpu.make_async_copy(source, cen_out.at[q * block : (q + 1) * block, :], sems.at[q])
-        copy.start()
-        copies.append(copy)
-        lw_out[q] = lw_ref[owner]
+        source = c_hbm.at[pl.ds(pl.multiple_of((me ^ o) * block, block), block), :]
+        target = cen_out.at[q * block : (q + 1) * block, :]
+        copies.append(pltpu.make_async_copy(source, target, sems.at[q]))
     return copies
 
 
@@ -85,8 +79,11 @@
     @pl.when(pl.program_id(0) == 0)
     def _():
         total[...] = jnp.zeros_like(total)
-        for copy in gather(n, offsets, block, c_hbm, lws_ref, cen_out, lw_out, sems):
-            copy.wait()
+        for copy in gather(n, offsets, block, c_hbm, cen_out, sems):
+            copy.start()
+        me = lax.rem(lax.axis_index("rows"), n)
+        for q, o in enumerate(offsets):
+            lw_out[q] = lws_ref[me ^ o]
 
     shift = column(lw_ref[0])
     half = a_ref.shape[0]
@@ -105,6 +102,8 @@
         for rows, out in ((a_ref, out_a), (b_ref, out_b)):
             out[:half, :] = rows[...]
             out[half:, : tail.shape[1]] = tail
+        for copy in gather(n, offsets, block, c_hbm, cen_out, sems):
+            copy.wait()
 
 
 def denominators(cen, lw, ua, ub, n, offsets):
@@ -136,7 +135,7 @@
             pltpu.VMEM((1, 2 * half), F32),
             pltpu.SemaphoreType.DMA((len(offsets),)),
         ],
-        compiler_params=params(DENOM_MIB),
+        compiler_params=params(40),
         cost_estimate=cost(2 * half * comps * dim, 2 * (comps + 2 * half) * dim, 2 * half * comps),
         name="denominators",
     )(cen, lw.reshape(comps // tile, 1, tile), cen, lw.reshape(n, 1, block), ua, ub)
@@ -212,18 +211,39 @@
     )(*args)
 
 
-def merge_kernel(terms, finish, n_in, *refs):
+def merge_kernel(terms, n_in, *refs):
     arrays, outs = refs[:n_in], refs[n_in:]
     for out, parts in zip(outs, terms):
         total = sum(arrays[i][at : at + out.shape[0], :].astype(F32) for i, at in parts)
-        out[...] = finish(total).astype(out.dtype)
+        out[...] = total.astype(out.dtype)
 
 
 def normalize(x):
     return x * lax.rsqrt(jnp.sum(x * x, 1, keepdims=True) + EPS)
 
 
-def merge(wanted, size, finish, name):
+def directions_kernel(terms, size, *refs):
+    *arrays, out = refs
+    for k, parts in enumerate(terms):
+        total = sum(arrays[i][at : at + size, :].astype(F32) for i, at in parts)
+        out[k * size : (k + 1) * size, :] = normalize(total).astype(out.dtype)
+
+
+def directions(wanted, size):
+    arrays, terms = distinct(wanted)
+    dim = arrays[0].shape[1]
+    return pl.pallas_call(
+        functools.partial(directions_kernel, terms, size),
+        out_shape=jax.ShapeDtypeStruct((size * len(wanted), dim), BF16),
+        in_specs=[VMEM] * len(arrays),
+        out_specs=VMEM,
+        compiler_params=params(8),
+        cost_estimate=cost(0, 12 * size * dim * len(wanted), size),
+        name="directions",
+    )(*arrays)
+
+
+def distinct(wanted):
     arrays, terms = [], []
     for parts in wanted:
         term = []
@@ -232,16 +252,20 @@
                 arrays.append(x)
             term.append((next(i for i, y in enumerate(arrays) if y is x), at))
         terms.append(term)
+    return arrays, terms
+
+
+def merge(wanted, sizes):
+    arrays, terms = distinct(wanted)
     dim = arrays[0].shape[1]
-    out = jax.ShapeDtypeStruct((size, dim), BF16)
-    return pl.pallas_call(
-        functools.partial(merge_kernel, terms, finish, len(arrays)),
-        out_shape=(out,) * len(wanted),
+    return pl.pallas_call(
+        functools.partial(merge_kernel, terms, len(arrays)),
+        out_shape=tuple(jax.ShapeDtypeStruct((size, dim), BF16) for size in sizes),
         in_specs=[VMEM] * len(arrays),
         out_specs=(VMEM,) * len(wanted),
-        compiler_params=params(16),
-        cost_estimate=cost(0, 12 * size * dim * len(wanted), size),
-        name=name,
+        compiler_params=params(8),
+        cost_estimate=cost(0, 12 * sum(sizes) * dim, sum(sizes)),
+        name="merge",
     )(*arrays)
 
 
@@ -251,7 +275,13 @@
     pieces, refs = refs[: 2 * n_rows], refs[2 * n_rows :]
     before, outs = refs[:-n_rows], refs[-n_rows:]
     c = jnp.concatenate([r[...] for r in comps], 0)
-    shift = jnp.concatenate([column(lw_ref[q : q + 1, :]) for q in lw_rows], 0)
+    shift = jnp.concatenate(
+        [
+            column(lw_ref[q : q + 1, :])[h * r.shape[0] : (h + 1) * r.shape[0], :]
+            for r, (q, h) in zip(comps, lw_rows)
+        ],
+        0,
+    )
     for i, out in enumerate(outs):
         for k in range(2):
             s = jnp.concatenate(
@@ -275,7 +305,7 @@
         out_shape=(jax.ShapeDtypeStruct((1, 2 * half), F32),) * n_rows,
         in_specs=[VMEM] * len(args),
         out_specs=(VMEM,) * n_rows,
-        compiler_params=params(24),
+        compiler_params=params(12),
         cost_estimate=cost(rows * n_comps * dim, 2 * (n_comps + rows) * dim, rows * n_comps),
         name="normalizers",
     )(*args)
@@ -291,6 +321,11 @@
     across, along = 1 << ACROSS, 1 << ALONG
     far = [1 << b for b in range(n.bit_length() - 1) if b not in (ACROSS, ALONG)]
 
+    def after(terms, ready):
+        *others, (x, at) = terms
+        x, _ = lax.optimization_barrier((x, ready))
+        return [*others, (x, at)]
+
     def swap(x, mask):
         return lax.ppermute(x, "rows", [(i, i ^ mask) for i in range(n)])
 
@@ -322,61 +357,82 @@
         for q in range(quarter):
             for h in range(PARTS):
                 parts[offsets[first + q], h] = [(x, q * block + h * sub) for x in pair]
+    ready, done = None, []
     for k, mask in list(enumerate(far))[1:]:
         leaving = [o for o in reversed(offsets) if (o, 0) in parts and o & mask]
         items = [(o, h) for o in leaving for h in range(PARTS)]
+        if k == 1 < len(far) - 1:
+            items = [(o, h) for o, h in items if o != mask or h == 0]
         for group in [items] if k == 1 else [[i] for i in items]:
-            merged = merge([parts.pop(i) for i in group], sub, lambda x: x, "merge")
-            for (o, h), x in zip(group, merged):
-                parts[o ^ mask, h].append((swap(x, mask), 0))
+            sizes = [block if o == mask and k == 1 < len(far) - 1 else sub for o, h in group]
+            wanted = [parts[i] for i in group]
+            if ready is not None:
+                wanted[0] = after(wanted[0], ready)
+            merged = merge(wanted, sizes)
+            done.append(merged[0])
+            if k > 1:
+                ready = merged[0]
+            for (o, h), x, size in zip(group, merged, sizes):
+                x = swap(x, mask)
+                for i in range(size // sub):
+                    parts.pop((o, h + i))
+                    parts[o ^ mask, h + i].append((x, i * sub))
     dirs = {}
     for h in range(PARTS):
-        (dirs[0, h],) = merge([parts[0, h]], sub, normalize, "directions")
+        wanted = parts[0, h] if h == 0 else after(parts[0, h], dirs[0, h - 1])
+        dirs[0, h] = directions([wanted], sub)
     own_dirs = jnp.concatenate([dirs[0, h] for h in range(PARTS)])
 
     counts = jnp.concatenate([keep_counts, send_counts])
-    for mask in far:
+    points = [done[0], done[min(1, len(done) - 1)], dirs[0, 0]]
+    for k, mask in enumerate(far):
+        counts, _ = lax.optimization_barrier((counts, points[min(k, 2)]))
         order = [where[o ^ mask] for o in offsets]
         got = swap(counts, mask)
         counts = counts + jnp.concatenate([got[q : q + 1] for q in order])
     new_lw = jnp.log(counts / row_total)
     own_lw = new_lw[0]
 
+    halves = range(PARTS)
     for mask in reversed(far[2:]):
         for o, h in list(dirs):
             dirs[o | mask, h] = swap(dirs[o, h], mask)
     pieces = (va, vb, xa, xb, za, zb, da, db)
     total = ()
 
-    def arrived(os):
-        return [dirs[o, h] for o in os for h in range(PARTS)]
-
-    def send_all(os, mask, after=None):
-        for o in os:
-            for h in range(PARTS):
-                x = dirs[o, h]
-                if after is not None:
-                    x, _ = lax.optimization_barrier((x, after))
-                    dirs[o, h] = x
-                dirs[o | mask, h] = swap(x, mask)
-
-    def use(o, total):
-        now = [o, o | far[0]]
-        return normalizers(arrived(now), new_lw, [where[o] for o in now], total, pieces, half)
+    def send(o, h, mask, ready=None):
+        x = dirs[o, h]
+        if ready is not None:
+            x, _ = lax.optimization_barrier((x, ready))
+            dirs[o, h] = x
+        dirs[o | mask, h] = swap(x, mask)
+
+    def use(o, hs, total):
+        keys = [(p, h) for p in (o, o | far[0]) for h in hs]
+        places = [(where[p], h) for p, h in keys]
+        return normalizers([dirs[k] for k in keys], new_lw, places, total, pieces, half)
 
     near, *outer = [o for o in offsets if not o & (far[0] | far[1])]
-    send_all([near], far[1])
-    send_all([near], far[0])
-    total = use(near, total)
-    send_all(outer, far[1], total[0])
-    send_all([near | far[1]], far[0], dirs[outer[0], 0] if outer else None)
-    send_all(outer, far[0])
-    for o in [near | far[1], *outer]:
-        total = use(o, total)
-    last = [o | far[1] for o in outer]
-    send_all(last, far[0], total[0])
-    for o in last:
-        total = use(o, total)
+    for h in halves:
+        send(near, h, far[1])
+        send(near, h, far[0])
+    total = use(near, halves, total)
+    for o in outer:
+        for h in halves:
+            send(o, h, far[1], total[0] if h == 0 else dirs[o | far[0], h - 1])
+            send(o, h, far[0])
+    for h in halves:
+        send(near | far[1], h, far[0], dirs[outer[0], 0] if outer else None)
+    total = use(near | far[1], halves, total)
+    for o in outer:
+        first, total = lax.optimization_barrier((dirs[o | far[1], 0], total))
+        dirs[o | far[1], 0] = first
+        send(o | far[1], 0, far[0])
+        total = use(o, halves, total)
+    for o in outer:
+        for h in halves[1:]:
+            send(o | far[1], h, far[0], total[0])
+        total = use(o | far[1], halves, total)
 
     own, x, z, d = total
     whole = own + swap(d, across | along) + swap(z, along) + swap(x, across)

time: 105 us -> 101 us (0.962)
  waiting for transfers between devices: 46 us -> 32 us
  starting transfers between devices: 23.7 us -> 30.7 us
  Pallas kernels: 24.9 us -> 27.3 us
    ppermute x25 -> x34, waiting for transfers between devices: 46 us -> 32 us  [swap(): return lax.ppermute(x, 'rows', [(i, i ^ mask) for i in range(n)])]
    ppermute x25 -> x34, starting transfers between devices: 23.7 us -> 30.7 us  [swap(): return lax.ppermute(x, 'rows', [(i, i ^ mask) for i in range(n)])]
    pallas_call x4, Pallas kernels: 6.01 us -> 8.93 us  [normalizers(): pl.pallas_call(functools.partial(normalizer_kernel, len(comps), lw_rows,...]
  transfers between devices with their start and end apart: 25 -> 34, of which waited for: 12 -> 13; matrix products, arithmetic and copies ran while one was open for 1% -> 1% of each run, Pallas kernels for 21% -> 24%
where the time goes in v3:
time: 101 us; the launch traced here: 100 us
  waiting for transfers between devices  32 us (32%)
  starting transfers between devices  30.7 us (30%)
  Pallas kernels  27.3 us (27%)
  local copies, waits for them, and re-layouts  7.98 us (8%)
  other arithmetic  1.35 us (1%)
    ppermute x34, waiting for transfers between devices, swap(): return lax.ppermute(x, 'rows', [(i, i ^ mask) for i in range(n)])  32 us
    ppermute x34, starting transfers between devices, swap(): return lax.ppermute(x, 'rows', [(i, i ^ mask) for i in range(n)])  30.7 us
    pallas_call x5, Pallas kernels, sums(): pl.pallas_call(functools.partial(sums_kernel, first, last, half, at), out...  10.8 us
    pallas_call x4, Pallas kernels, normalizers(): pl.pallas_call(functools.partial(normalizer_kernel, len(comps), lw_rows,...  8.93 us
    unnamed x16, local copies, waits for them, and re-layouts  7.43 us
    pallas_call x1, Pallas kernels, denominators(): pl.pallas_call(functools.partial(denom_kernel, n, offsets), grid=(comps /...  6.8 us
  transfers between devices with their start and end apart: 34, of which 13 were waited for; matrix products, arithmetic and copies ran while one was open for 1% of the time, Pallas kernels for 24%

profile of v3, /device:TPU:0, one launch (start us, length us, event | category | flops | bytes accessed | tf_op | source)
XLA Modules:
  0.0 100.2 jit_solution(9643552473054465598)
XLA Ops:
  2.2 3.0 %collective-permute-start.4 = (bf16[256,1024]{1,0:T(8,128)(2,1)S(1)}, bf16[256,1024]{1,0:T(8,128)(2,1)S(1)}, u32[]{:S(2)}, u32[]{:S(2)}) collective-permute-start(bf16[256,1024]{1,0:T(8,128)(2,1)S(1)} %get-tuple-element.56.b_ref), channel_id=1, source_target_pairs={{0,2},{1,3},{2,0},{3,1},{4,6},{5,7},{6,4},{7,5},{8,10},{9,11},{10,... | collective-permute-start | bytes 1572872 | tf_op jit(solution)/shard_map/ppermute | solution.py:330
  5.2 1.6 %collective-permute-start.2 = (bf16[256,1024]{1,0:T(8,128)(2,1)S(1)}, bf16[256,1024]{1,0:T(8,128)(2,1)S(1)}, u32[]{:S(2)}, u32[]{:S(2)}) collective-permute-start(bf16[256,1024]{1,0:T(8,128)(2,1)S(1)} %get-tuple-element.55.a_ref), channel_id=1, source_target_pairs={{0,8},{1,9},{2,10},{3,11},{4,12},{5,13},{6,14},{7,15},{8,0},{9,1},... | collective-permute-start | bytes 1572872 | tf_op jit(solution)/shard_map/ppermute | solution.py:330
  6.8 3.4 %copy-done = bf16[4096,1024]{1,0:T(8,128)(2,1)S(1)} copy-done((bf16[4096,1024]{1,0:T(8,128)(2,1)S(1)}, bf16[4096,1024]{1,0:T(8,128)(2,1)}, u32[]{:S(2)}) %copy-start) | copy-done | bytes 8388632
  10.9 6.8 %denominators.1 = (bf16[272,1024]{1,0:T(8,128)(2,1)S(1)}, bf16[272,1024]{1,0:T(8,128)(2,1)S(1)}, bf16[1024,1024]{1,0:T(8,128)(2,1)S(1)}, f32[8,1,128]{2,1,0:T(1,128)S(1)}) custom-call(bf16[4096,1024]{1,0:T(8,128)(2,1)S(1)} %copy-done, f32[8,1,512]{2,1,0:T(1,128)S(1)} %bitcast.5, bf16[4096,1024]{1,0:T(8,128)(2,1)S(1)} %copy-done, f32[32,1,128]{2,1,0:T(1,128)S(1)} %bitcast.6, ...), custom_call_target="tpu_custom_call" | custom-call | flops 4294967296 | bytes 9437184 | tf_op jit(solution)/shard_map/denominators/pallas_call | solution.py:121
  18.6 1.7 %collective-permute-start.3 = (bf16[256,1024]{1,0:T(8,128)(2,1)S(1)}, bf16[256,1024]{1,0:T(8,128)(2,1)S(1)}, u32[]{:S(2)}, u32[]{:S(2)}) collective-permute-start(bf16[256,1024]{1,0:T(8,128)(2,1)S(1)} %collective-permute-done.2.refs_0_.refs_9_), channel_id=1, source_target_pairs={{0,2},{1,3},{2,0},{3,1},{4,6},{5,7},{6,4},{7,5},{8,10},{9,11},{10,... | collective-permute-start | bytes 1572872 | tf_op jit(solution)/shard_map/ppermute | solution.py:330
  20.2 1.6 %collective-permute-start.5 = (bf16[256,1024]{1,0:T(8,128)(2,1)S(1)}, bf16[256,1024]{1,0:T(8,128)(2,1)S(1)}, u32[]{:S(2)}, u32[]{:S(2)}) collective-permute-start(bf16[256,1024]{1,0:T(8,128)(2,1)S(1)} %collective-permute-done.4.refs_1_.refs_8_), channel_id=1, source_target_pairs={{0,8},{1,9},{2,10},{3,11},{4,12},{5,13},{6,14},{7,15},{8,0},{9,1},... | collective-permute-start | bytes 1572872 | tf_op jit(solution)/shard_map/ppermute | solution.py:330
  21.8 2.5 %sums.5 = (f32[1024,1024]{1,0:T(8,128)S(1)}, f32[1024,128]{1,0:T(8,128)S(1)}) custom-call(bf16[1024,1024]{1,0:T(8,128)(2,1)S(1)} %get-tuple-element.57.c_ref, f32[8,1,128]{2,1,0:T(1,128)S(1)} %get-tuple-element.58.lw_ref, bf16[272,1024]{1,0:T(8,128)(2,1)S(1)} %get-tuple-element.60.tail_ref.refs_0_.refs_5_, ...), custom_call_target="tpu_custom_call" | custom-call | flops 2147483648 | bytes 3145728 | tf_op jit(solution)/shard_map/sums/pallas_call | solution.py:202
  24.4 9.0 %collective-permute-done.tail_ref.refs_1_.refs_10_ = bf16[272,1024]{1,0:T(8,128)(2,1)S(1)} collective-permute-done((bf16[272,1024]{1,0:T(8,128)(2,1)S(1)}, bf16[272,1024]{1,0:T(8,128)(2,1)S(1)}, u32[]{:S(2)}, u32[]{:S(2)}) %collective-permute-start) | collective-permute-done | bytes 557088 | tf_op jit(solution)/shard_map/ppermute | solution.py:330
  33.9 2.7 %sums.6 = (f32[1024,1024]{1,0:T(8,128)S(1)}, f32[1024,128]{1,0:T(8,128)S(1)}) custom-call(bf16[1024,1024]{1,0:T(8,128)(2,1)S(1)} %get-tuple-element.57.c_ref, f32[8,1,128]{2,1,0:T(1,128)S(1)} %get-tuple-element.58.lw_ref, bf16[272,1024]{1,0:T(8,128)(2,1)S(1)} %collective-permute-done.6.tail_ref.refs_0_.refs_7_, ...), custom_call_target="tpu_custom_call", output_to_operand_aliasing={{0}: (5, {}), {1}: (6, {})} | custom-call | flops 2147483648 | bytes 3145728 | tf_op jit(solution)/shard_map/sums/pallas_call | solution.py:202
  36.6 2.7 %sums.7 = (f32[1024,1024]{1,0:T(8,128)S(1)}, f32[1024,128]{1,0:T(8,128)S(1)}) custom-call(bf16[1024,1024]{1,0:T(8,128)(2,1)S(1)} %get-tuple-element.57.c_ref, f32[8,1,128]{2,1,0:T(1,128)S(1)} %get-tuple-element.58.lw_ref, bf16[272,1024]{1,0:T(8,128)(2,1)S(1)} %collective-permute-done.tail_ref.refs_1_.refs_10_, ...), custom_call_target="tpu_custom_call", output_to_operand_aliasing={{0}: (5, {}), {1}: (6, {})} | custom-call | flops 2147483648 | bytes 3145728 | tf_op jit(solution)/shard_map/sums/pallas_call | solution.py:202
  39.4 4.3 %collective-permute-done.1.tail_ref = bf16[16,1024]{1,0:T(8,128)(2,1)S(1)} collective-permute-done((bf16[16,1024]{1,0:T(8,128)(2,1)S(1)}, bf16[16,1024]{1,0:T(8,128)(2,1)S(1)}, u32[]{:S(2)}, u32[]{:S(2)}) %collective-permute-start.1) | collective-permute-done | bytes 32800 | tf_op jit(solution)/shard_map/ppermute | solution.py:330
  48.1 1.5 %collective-permute-start.10 = (bf16[64,1024]{1,0:T(8,128)(2,1)S(1)}, bf16[64,1024]{1,0:T(8,128)(2,1)S(1)}, u32[]{:S(2)}, u32[]{:S(2)}) collective-permute-start(bf16[64,1024]{1,0:T(8,128)(2,1)S(1)} %get-tuple-element.72), channel_id=1, source_target_pairs={{0,4},{1,5},{2,6},{3,7},{4,0},{5,1},{6,2},{7,3},{8,12},{9,13},{10,... | collective-permute-start | bytes 393224 | tf_op jit(solution)/shard_map/ppermute | solution.py:330
  50.2 4.3 %collective-permute-done.10.refs_2_ = bf16[64,1024]{1,0:T(8,128)(2,1)S(1)} collective-permute-done((bf16[64,1024]{1,0:T(8,128)(2,1)S(1)}, bf16[64,1024]{1,0:T(8,128)(2,1)S(1)}, u32[]{:S(2)}, u32[]{:S(2)}) %collective-permute-start.10) | collective-permute-done | bytes 131104 | tf_op jit(solution)/shard_map/ppermute | solution.py:330
  54.5 1.6 %collective-permute-start.15 = (f32[8,128]{1,0:T(8,128)S(1)}, f32[8,128]{1,0:T(8,128)S(1)}, u32[]{:S(2)}, u32[]{:S(2)}) collective-permute-start(f32[8,128]{1,0:T(8,128)S(1)} %maximum_add_fusion), channel_id=1, source_target_pairs={{0,4},{1,5},{2,6},{3,7},{4,0},{5,1},{6,2},{7,3},{8,12},{9,13},{10,... | collective-permute-start | bytes 12296 | tf_op jit(solution)/shard_map/ppermute | solution.py:330
  56.5 2.6 %collective-permute-start.11 = (bf16[64,1024]{1,0:T(8,128)(2,1)S(1)}, bf16[64,1024]{1,0:T(8,128)(2,1)S(1)}, u32[]{:S(2)}, u32[]{:S(2)}) collective-permute-start(bf16[64,1024]{1,0:T(8,128)(2,1)S(1)} %merge.4), channel_id=1, source_target_pairs={{0,16},{1,17},{2,18},{3,19},{4,20},{5,21},{6,22},{7,23},{8,24},{9,... | collective-permute-start | bytes 393224 | tf_op jit(solution)/shard_map/ppermute | solution.py:330
  59.6 3.4 %collective-permute-done.9.refs_2_ = bf16[128,1024]{1,0:T(8,128)(2,1)S(1)} collective-permute-done((bf16[128,1024]{1,0:T(8,128)(2,1)S(1)}, bf16[128,1024]{1,0:T(8,128)(2,1)S(1)}, u32[]{:S(2)}, u32[]{:S(2)}) %collective-permute-start.9) | collective-permute-done | bytes 262176 | tf_op jit(solution)/shard_map/ppermute | solution.py:330
  63.0 5.1 %collective-permute-done.11.refs_3_ = bf16[64,1024]{1,0:T(8,128)(2,1)S(1)} collective-permute-done((bf16[64,1024]{1,0:T(8,128)(2,1)S(1)}, bf16[64,1024]{1,0:T(8,128)(2,1)S(1)}, u32[]{:S(2)}, u32[]{:S(2)}) %collective-permute-start.11) | collective-permute-done | bytes 131104 | tf_op jit(solution)/shard_map/ppermute | solution.py:330
  68.4 2.8 %collective-permute-start.17 = (bf16[64,1024]{1,0:T(8,128)(2,1)S(1)}, bf16[64,1024]{1,0:T(8,128)(2,1)}, u32[]{:S(2)}, u32[]{:S(2)}) collective-permute-start(bf16[64,1024]{1,0:T(8,128)(2,1)S(1)} %directions.2.refs_0_), channel_id=1, source_target_pairs={{0,16},{1,17},{2,18},{3,19},{4,20},{5,21},{6,22},{7,23},{8,24},{9,... | collective-permute-start | bytes 393224 | tf_op jit(solution)/shard_map/ppermute | solution.py:330
  71.7 1.5 %collective-permute-start.22 = (bf16[64,1024]{1,0:T(8,128)(2,1)S(1)}, bf16[64,1024]{1,0:T(8,128)(2,1)}, u32[]{:S(2)}, u32[]{:S(2)}) collective-permute-start(bf16[64,1024]{1,0:T(8,128)(2,1)S(1)} %directions.3.refs_1_), channel_id=1, source_target_pairs={{0,4},{1,5},{2,6},{3,7},{4,0},{5,1},{6,2},{7,3},{8,12},{9,13},{10,... | collective-permute-start | bytes 393224 | tf_op jit(solution)/shard_map/ppermute | solution.py:330
  76.6 2.6 %normalizers.4 = (f32[1,512]{1,0:T(1,128)S(1)}, f32[1,512]{1,0:T(1,128)S(1)}, f32[1,512]{1,0:T(1,128)S(1)}, f32[1,512]{1,0:T(1,128)S(1)}) custom-call(bf16[64,1024]{1,0:T(8,128)(2,1)S(1)} %directions.2.refs_0_, bf16[64,1024]{1,0:T(8,128)(2,1)S(1)} %directions.3.refs_1_, bf16[64,1024]{1,0:T(8,128)(2,1)} %collective-permute-done.18.refs_2_, ...), custom_call_target="tpu_custom_call" | custom-call | flops 1073741824 | bytes 4718592 | tf_op jit(solution)/shard_map/normalizers/pallas_call | solution.py:303
  79.3 2.2 %collective-permute-done.17.refs_0_ = bf16[64,1024]{1,0:T(8,128)(2,1)} collective-permute-done((bf16[64,1024]{1,0:T(8,128)(2,1)S(1)}, bf16[64,1024]{1,0:T(8,128)(2,1)}, u32[]{:S(2)}, u32[]{:S(2)}) %collective-permute-start.17) | collective-permute-done | bytes 131104 | tf_op jit(solution)/shard_map/ppermute | solution.py:330
  83.9 1.5 %collective-permute-start.27 = (bf16[64,1024]{1,0:T(8,128)(2,1)S(1)}, bf16[64,1024]{1,0:T(8,128)(2,1)S(1)}, u32[]{:S(2)}, u32[]{:S(2)}) collective-permute-start(bf16[64,1024]{1,0:T(8,128)(2,1)S(1)} %collective-permute-done.25.refs_1_), channel_id=1, source_target_pairs={{0,4},{1,5},{2,6},{3,7},{4,0},{5,1},{6,2},{7,3},{8,12},{9,13},{10,... | collective-permute-start | bytes 393224 | tf_op jit(solution)/shard_map/ppermute | solution.py:330
  85.4 2.5 %normalizers.5 = (f32[1,512]{1,0:T(1,128)S(1)}, f32[1,512]{1,0:T(1,128)S(1)}, f32[1,512]{1,0:T(1,128)S(1)}, f32[1,512]{1,0:T(1,128)S(1)}) custom-call(bf16[64,1024]{1,0:T(8,128)(2,1)} %collective-permute-done.21.refs_0_, bf16[64,1024]{1,0:T(8,128)(2,1)} %collective-permute-done.22.refs_1_, bf16[64,1024]{1,0:T(8,128)(2,1)S(1)} %collective-permute-done.23.refs_2_, ...), custom_call_target="tpu_custom_call" | custom-call | flops 1073741824 | bytes 4718592 | tf_op jit(solution)/shard_map/normalizers/pallas_call | solution.py:303
  88.6 2.4 %normalizers.6 = (f32[1,512]{1,0:T(1,128)S(1)}, f32[1,512]{1,0:T(1,128)S(1)}, f32[1,512]{1,0:T(1,128)S(1)}, f32[1,512]{1,0:T(1,128)S(1)}) custom-call(bf16[64,1024]{1,0:T(8,128)(2,1)} %collective-permute-done.17.refs_0_, bf16[64,1024]{1,0:T(8,128)(2,1)S(1)} %collective-permute-done.25.refs_1_, bf16[64,1024]{1,0:T(8,128)(2,1)S(1)} %collective-permute-done.26.refs_2_, ...), custom_call_target="tpu_custom_call" | custom-call | flops 1073741824 | bytes 4718592 | tf_op jit(solution)/shard_map/normalizers/pallas_call | solution.py:303
  (88 shorter events, 26.1 us)
Async XLA Ops:
  2.2 18.1 %collective-permute-start.4 = (bf16[256,1024]{1,0:T(8,128)(2,1)S(1)}, bf16[256,1024]{1,0:T(8,128)(2,1)S(1)}, u32[]{:S(2)}, u32[]{:S(2)}) collective-permute-start(bf16[256,1024]{1,0:T(8,128)(2,1)S(1)} %get-tuple-element.56.b_ref), channel_id=1, source_target_pairs={{0,2},{1,3},{2,0},{3,1},{4,6},{5,7},{6,4},{7,5},{8,10},{9,11},{10,... | collective-permute-start | bytes 1572872 | tf_op jit(solution)/shard_map/ppermute | solution.py:330
  5.2 13.4 %collective-permute-start.2 = (bf16[256,1024]{1,0:T(8,128)(2,1)S(1)}, bf16[256,1024]{1,0:T(8,128)(2,1)S(1)}, u32[]{:S(2)}, u32[]{:S(2)}) collective-permute-start(bf16[256,1024]{1,0:T(8,128)(2,1)S(1)} %get-tuple-element.55.a_ref), channel_id=1, source_target_pairs={{0,8},{1,9},{2,10},{3,11},{4,12},{5,13},{6,14},{7,15},{8,0},{9,1},... | collective-permute-start | bytes 1572872 | tf_op jit(solution)/shard_map/ppermute | solution.py:330
  17.7 15.6 %collective-permute-start = (bf16[272,1024]{1,0:T(8,128)(2,1)S(1)}, bf16[272,1024]{1,0:T(8,128)(2,1)S(1)}, u32[]{:S(2)}, u32[]{:S(2)}) collective-permute-start(bf16[272,1024]{1,0:T(8,128)(2,1)S(1)} %get-tuple-element.59.refs_1_.refs_6_), channel_id=1, source_target_pairs={{0,8},{1,9},{2,10},{3,11},{4,12},{5,13},{6,14},{7,15},{8,0},{9,1},... | collective-permute-start | bytes 1671176 | tf_op jit(solution)/shard_map/ppermute | solution.py:330
  18.2 15.7 %collective-permute-start.6 = (bf16[272,1024]{1,0:T(8,128)(2,1)S(1)}, bf16[272,1024]{1,0:T(8,128)(2,1)S(1)}, u32[]{:S(2)}, u32[]{:S(2)}) collective-permute-start(bf16[272,1024]{1,0:T(8,128)(2,1)S(1)} %get-tuple-element.60.tail_ref.refs_0_.refs_5_), channel_id=1, source_target_pairs={{0,2},{1,3},{2,0},{3,1},{4,6},{5,7},{6,4},{7,5},{8,10},{9,11},{10,... | collective-permute-start | bytes 1671176 | tf_op jit(solution)/shard_map/ppermute | solution.py:330
  18.6 25.1 %collective-permute-start.3 = (bf16[256,1024]{1,0:T(8,128)(2,1)S(1)}, bf16[256,1024]{1,0:T(8,128)(2,1)S(1)}, u32[]{:S(2)}, u32[]{:S(2)}) collective-permute-start(bf16[256,1024]{1,0:T(8,128)(2,1)S(1)} %collective-permute-done.2.refs_0_.refs_9_), channel_id=1, source_target_pairs={{0,2},{1,3},{2,0},{3,1},{4,6},{5,7},{6,4},{7,5},{8,10},{9,11},{10,... | collective-permute-start | bytes 1572872 | tf_op jit(solution)/shard_map/ppermute | solution.py:330
  20.2 23.4 %collective-permute-start.5 = (bf16[256,1024]{1,0:T(8,128)(2,1)S(1)}, bf16[256,1024]{1,0:T(8,128)(2,1)S(1)}, u32[]{:S(2)}, u32[]{:S(2)}) collective-permute-start(bf16[256,1024]{1,0:T(8,128)(2,1)S(1)} %collective-permute-done.4.refs_1_.refs_8_), channel_id=1, source_target_pairs={{0,8},{1,9},{2,10},{3,11},{4,12},{5,13},{6,14},{7,15},{8,0},{9,1},... | collective-permute-start | bytes 1572872 | tf_op jit(solution)/shard_map/ppermute | solution.py:330
  33.3 10.3 %collective-permute-start.1 = (bf16[16,1024]{1,0:T(8,128)(2,1)S(1)}, bf16[16,1024]{1,0:T(8,128)(2,1)S(1)}, u32[]{:S(2)}, u32[]{:S(2)}) collective-permute-start(bf16[16,1024]{1,0:T(8,128)(2,1)S(1)} %slice.80), channel_id=1, source_target_pairs={{0,2},{1,3},{2,0},{3,1},{4,6},{5,7},{6,4},{7,5},{8,10},{9,11},{10,... | collective-permute-start | bytes 98312 | tf_op jit(solution)/shard_map/ppermute | solution.py:330
  45.1 5.0 %collective-permute-start.7 = (f32[256,1024]{1,0:T(8,128)S(1)}, f32[256,1024]{1,0:T(8,128)S(1)}, u32[]{:S(2)}, u32[]{:S(2)}) collective-permute-start(f32[256,1024]{1,0:T(8,128)S(1)} %get-tuple-element.68), channel_id=1, source_target_pairs={{0,1},{1,0},{2,3},{3,2},{4,5},{5,4},{6,7},{7,6},{8,9},{9,8},{10,11... | collective-permute-start | bytes 3145736 | tf_op jit(solution)/shard_map/ppermute | solution.py:330
  48.1 6.3 %collective-permute-start.10 = (bf16[64,1024]{1,0:T(8,128)(2,1)S(1)}, bf16[64,1024]{1,0:T(8,128)(2,1)S(1)}, u32[]{:S(2)}, u32[]{:S(2)}) collective-permute-start(bf16[64,1024]{1,0:T(8,128)(2,1)S(1)} %get-tuple-element.72), channel_id=1, source_target_pairs={{0,4},{1,5},{2,6},{3,7},{4,0},{5,1},{6,2},{7,3},{8,12},{9,13},{10,... | collective-permute-start | bytes 393224 | tf_op jit(solution)/shard_map/ppermute | solution.py:330
  49.6 9.5 %collective-permute-start.12 = (bf16[64,1024]{1,0:T(8,128)(2,1)S(1)}, bf16[64,1024]{1,0:T(8,128)(2,1)S(1)}, u32[]{:S(2)}, u32[]{:S(2)}) collective-permute-start(bf16[64,1024]{1,0:T(8,128)(2,1)S(1)} %get-tuple-element.73), channel_id=1, source_target_pairs={{0,4},{1,5},{2,6},{3,7},{4,0},{5,1},{6,2},{7,3},{8,12},{9,13},{10,... | collective-permute-start | bytes 393224 | tf_op jit(solution)/shard_map/ppermute | solution.py:330
  54.5 5.1 %collective-permute-start.15 = (f32[8,128]{1,0:T(8,128)S(1)}, f32[8,128]{1,0:T(8,128)S(1)}, u32[]{:S(2)}, u32[]{:S(2)}) collective-permute-start(f32[8,128]{1,0:T(8,128)S(1)} %maximum_add_fusion), channel_id=1, source_target_pairs={{0,4},{1,5},{2,6},{3,7},{4,0},{5,1},{6,2},{7,3},{8,12},{9,13},{10,... | collective-permute-start | bytes 12296 | tf_op jit(solution)/shard_map/ppermute | solution.py:330
  56.0 7.0 %collective-permute-start.9 = (bf16[128,1024]{1,0:T(8,128)(2,1)S(1)}, bf16[128,1024]{1,0:T(8,128)(2,1)S(1)}, u32[]{:S(2)}, u32[]{:S(2)}) collective-permute-start(bf16[128,1024]{1,0:T(8,128)(2,1)S(1)} %get-tuple-element.71), channel_id=1, source_target_pairs={{0,4},{1,5},{2,6},{3,7},{4,0},{5,1},{6,2},{7,3},{8,12},{9,13},{10,... | collective-permute-start | bytes 786440 | tf_op jit(solution)/shard_map/ppermute | solution.py:330
  56.5 11.5 %collective-permute-start.11 = (bf16[64,1024]{1,0:T(8,128)(2,1)S(1)}, bf16[64,1024]{1,0:T(8,128)(2,1)S(1)}, u32[]{:S(2)}, u32[]{:S(2)}) collective-permute-start(bf16[64,1024]{1,0:T(8,128)(2,1)S(1)} %merge.4), channel_id=1, source_target_pairs={{0,16},{1,17},{2,18},{3,19},{4,20},{5,21},{6,22},{7,23},{8,24},{9,... | collective-permute-start | bytes 393224 | tf_op jit(solution)/shard_map/ppermute | solution.py:330
  59.2 12.1 %collective-permute-start.13 = (bf16[64,1024]{1,0:T(8,128)(2,1)S(1)}, bf16[64,1024]{1,0:T(8,128)(2,1)S(1)}, u32[]{:S(2)}, u32[]{:S(2)}) collective-permute-start(bf16[64,1024]{1,0:T(8,128)(2,1)S(1)} %merge.5), channel_id=1, source_target_pairs={{0,16},{1,17},{2,18},{3,19},{4,20},{5,21},{6,22},{7,23},{8,24},{9,... | collective-permute-start | bytes 393224 | tf_op jit(solution)/shard_map/ppermute | solution.py:330
  68.2 5.0 %collective-permute-start.16 = (f32[8,128]{1,0:T(8,128)S(1)}, f32[8,128]{1,0:T(8,128)S(1)}, u32[]{:S(2)}, u32[]{:S(2)}) collective-permute-start(f32[8,128]{1,0:T(8,128)S(1)} %maximum_add_fusion.1), channel_id=1, source_target_pairs={{0,16},{1,17},{2,18},{3,19},{4,20},{5,21},{6,22},{7,23},{8,24},{9,... | collective-permute-start | bytes 12296 | tf_op jit(solution)/shard_map/ppermute | solution.py:330
  68.3 6.2 %collective-permute-start.18 = (bf16[64,1024]{1,0:T(8,128)(2,1)S(1)}, bf16[64,1024]{1,0:T(8,128)(2,1)}, u32[]{:S(2)}, u32[]{:S(2)}) collective-permute-start(bf16[64,1024]{1,0:T(8,128)(2,1)S(1)} %directions.2.refs_0_), channel_id=1, source_target_pairs={{0,1},{1,0},{2,3},{3,2},{4,5},{5,4},{6,7},{7,6},{8,9},{9,8},{10,11... | collective-permute-start | bytes 393224 | tf_op jit(solution)/shard_map/ppermute | solution.py:330
  68.4 13.1 %collective-permute-start.17 = (bf16[64,1024]{1,0:T(8,128)(2,1)S(1)}, bf16[64,1024]{1,0:T(8,128)(2,1)}, u32[]{:S(2)}, u32[]{:S(2)}) collective-permute-start(bf16[64,1024]{1,0:T(8,128)(2,1)S(1)} %directions.2.refs_0_), channel_id=1, source_target_pairs={{0,16},{1,17},{2,18},{3,19},{4,20},{5,21},{6,22},{7,23},{8,24},{9,... | collective-permute-start | bytes 393224 | tf_op jit(solution)/shard_map/ppermute | solution.py:330
  71.7 9.8 %collective-permute-start.22 = (bf16[64,1024]{1,0:T(8,128)(2,1)S(1)}, bf16[64,1024]{1,0:T(8,128)(2,1)}, u32[]{:S(2)}, u32[]{:S(2)}) collective-permute-start(bf16[64,1024]{1,0:T(8,128)(2,1)S(1)} %directions.3.refs_1_), channel_id=1, source_target_pairs={{0,4},{1,5},{2,6},{3,7},{4,0},{5,1},{6,2},{7,3},{8,12},{9,13},{10,... | collective-permute-start | bytes 393224 | tf_op jit(solution)/shard_map/ppermute | solution.py:330
  73.2 8.8 %collective-permute-start.21 = (bf16[64,1024]{1,0:T(8,128)(2,1)S(1)}, bf16[64,1024]{1,0:T(8,128)(2,1)}, u32[]{:S(2)}, u32[]{:S(2)}) collective-permute-start(bf16[64,1024]{1,0:T(8,128)(2,1)S(1)} %directions.2.refs_0_), channel_id=1, source_target_pairs={{0,4},{1,5},{2,6},{3,7},{4,0},{5,1},{6,2},{7,3},{8,12},{9,13},{10,... | collective-permute-start | bytes 393224 | tf_op jit(solution)/shard_map/ppermute | solution.py:330
  74.4 9.4 %collective-permute-start.25 = (bf16[64,1024]{1,0:T(8,128)(2,1)S(1)}, bf16[64,1024]{1,0:T(8,128)(2,1)S(1)}, u32[]{:S(2)}, u32[]{:S(2)}) collective-permute-start(bf16[64,1024]{1,0:T(8,128)(2,1)S(1)} %directions.3.refs_1_), channel_id=1, source_target_pairs={{0,16},{1,17},{2,18},{3,19},{4,20},{5,21},{6,22},{7,23},{8,24},{9,... | collective-permute-start | bytes 393224 | tf_op jit(solution)/shard_map/ppermute | solution.py:330
  82.1 6.5 %collective-permute-start.20 = (bf16[64,1024]{1,0:T(8,128)(2,1)}, bf16[64,1024]{1,0:T(8,128)(2,1)S(1)}, u32[]{:S(2)}, u32[]{:S(2)}) collective-permute-start(bf16[64,1024]{1,0:T(8,128)(2,1)} %collective-permute-done.17.refs_0_), channel_id=1, source_target_pairs={{0,4},{1,5},{2,6},{3,7},{4,0},{5,1},{6,2},{7,3},{8,12},{9,13},{10,... | collective-permute-start | bytes 393224 | tf_op jit(solution)/shard_map/ppermute | solution.py:330
  83.9 4.7 %collective-permute-start.28 = (bf16[64,1024]{1,0:T(8,128)(2,1)S(1)}, bf16[64,1024]{1,0:T(8,128)(2,1)S(1)}, u32[]{:S(2)}, u32[]{:S(2)}) collective-permute-start(bf16[64,1024]{1,0:T(8,128)(2,1)S(1)} %collective-permute-done.25.refs_1_), channel_id=1, source_target_pairs={{0,1},{1,0},{2,3},{3,2},{4,5},{5,4},{6,7},{7,6},{8,9},{9,8},{10,11... | collective-permute-start | bytes 393224 | tf_op jit(solution)/shard_map/ppermute | solution.py:330
  83.9 7.1 %collective-permute-start.27 = (bf16[64,1024]{1,0:T(8,128)(2,1)S(1)}, bf16[64,1024]{1,0:T(8,128)(2,1)S(1)}, u32[]{:S(2)}, u32[]{:S(2)}) collective-permute-start(bf16[64,1024]{1,0:T(8,128)(2,1)S(1)} %collective-permute-done.25.refs_1_), channel_id=1, source_target_pairs={{0,4},{1,5},{2,6},{3,7},{4,0},{5,1},{6,2},{7,3},{8,12},{9,13},{10,... | collective-permute-start | bytes 393224 | tf_op jit(solution)/shard_map/ppermute | solution.py:330
  94.0 4.6 %collective-permute-start.31 = (f32[1,512]{1,0:T(1,128)S(1)}, f32[1,512]{1,0:T(1,128)S(1)}, u32[]{:S(2)}, u32[]{:S(2)}) collective-permute-start(f32[1,512]{1,0:T(1,128)S(1)} %get-tuple-element.104), channel_id=1, source_target_pairs={{0,10},{1,11},{2,8},{3,9},{4,14},{5,15},{6,12},{7,13},{8,2},{9,3},... | collective-permute-start | bytes 6152 | tf_op jit(solution)/shard_map/ppermute | solution.py:330
  (18 other events, 82.7 us)

commit v4 on v3

--- a/solution.py
+++ b/solution.py
@@ -407,10 +407,10 @@
             dirs[o, h] = x
         dirs[o | mask, h] = swap(x, mask)
 
-    def use(o, hs, total):
+    def use(o, hs, total, rows=None):
         keys = [(p, h) for p in (o, o | far[0]) for h in hs]
         places = [(where[p], h) for p, h in keys]
-        return normalizers([dirs[k] for k in keys], new_lw, places, total, pieces, half)
+        return normalizers([dirs[k] for k in keys], new_lw, places, total, rows or pieces, half)
 
     near, *outer = [o for o in offsets if not o & (far[0] | far[1])]
     for h in halves:
@@ -432,7 +432,9 @@
     for o in outer:
         for h in halves[1:]:
             send(o | far[1], h, far[0], total[0])
-        total = use(o | far[1], halves, total)
+        (own,), others = total[:1], total[1:]
+        others = use(o | far[1], halves, others, pieces[2:])
+        total = (*use(o | far[1], halves, (own,), pieces[:2]), *others)
 
     own, x, z, d = total
     whole = own + swap(d, across | along) + swap(z, along) + swap(x, across)

time: 101 us -> 101 us (level)
    pallas_call x4 -> x5, Pallas kernels: 8.93 us -> 9.15 us  [normalizers(): pl.pallas_call(functools.partial(normalizer_kernel, len(comps), lw_rows,...]
  transfers between devices with their start and end apart: 34 -> 34, of which waited for: 13 -> 13; matrix products, arithmetic and copies ran while one was open for 1% -> 1% of each run, Pallas kernels for 24% -> 25%
where the time goes in v4:
time: 101 us; the launch traced here: 100 us
  waiting for transfers between devices  32.1 us (32%)
  starting transfers between devices  30.4 us (30%)
  Pallas kernels  27.5 us (27%)
  local copies, waits for them, and re-layouts  7.99 us (8%)
  other arithmetic  1.36 us (1%)
    ppermute x34, waiting for transfers between devices, swap(): return lax.ppermute(x, 'rows', [(i, i ^ mask) for i in range(n)])  32.1 us
    ppermute x34, starting transfers between devices, swap(): return lax.ppermute(x, 'rows', [(i, i ^ mask) for i in range(n)])  30.4 us
    pallas_call x5, Pallas kernels, sums(): pl.pallas_call(functools.partial(sums_kernel, first, last, half, at), out...  10.8 us
    pallas_call x5, Pallas kernels, normalizers(): pl.pallas_call(functools.partial(normalizer_kernel, len(comps), lw_rows,...  9.15 us
    unnamed x16, local copies, waits for them, and re-layouts  7.43 us
    pallas_call x1, Pallas kernels, denominators(): pl.pallas_call(functools.partial(denom_kernel, n, offsets), grid=(comps /...  6.8 us
  transfers between devices with their start and end apart: 34, of which 13 were waited for; matrix products, arithmetic and copies ran while one was open for 1% of the time, Pallas kernels for 25%

profile of v4, /device:TPU:0, one launch (start us, length us, event | category | flops | bytes accessed | tf_op | source)
XLA Modules:
  0.0 100.2 jit_solution(11779081765631026697)
XLA Ops:
  2.2 3.0 %collective-permute-start.4 = (bf16[256,1024]{1,0:T(8,128)(2,1)S(1)}, bf16[256,1024]{1,0:T(8,128)(2,1)S(1)}, u32[]{:S(2)}, u32[]{:S(2)}) collective-permute-start(bf16[256,1024]{1,0:T(8,128)(2,1)S(1)} %get-tuple-element.55.b_ref), channel_id=1, source_target_pairs={{0,2},{1,3},{2,0},{3,1},{4,6},{5,7},{6,4},{7,5},{8,10},{9,11},{10,... | collective-permute-start | bytes 1572872 | tf_op jit(solution)/shard_map/ppermute | solution.py:330
  5.2 1.6 %collective-permute-start.2 = (bf16[256,1024]{1,0:T(8,128)(2,1)S(1)}, bf16[256,1024]{1,0:T(8,128)(2,1)S(1)}, u32[]{:S(2)}, u32[]{:S(2)}) collective-permute-start(bf16[256,1024]{1,0:T(8,128)(2,1)S(1)} %get-tuple-element.54.a_ref), channel_id=1, source_target_pairs={{0,8},{1,9},{2,10},{3,11},{4,12},{5,13},{6,14},{7,15},{8,0},{9,1},... | collective-permute-start | bytes 1572872 | tf_op jit(solution)/shard_map/ppermute | solution.py:330
  6.8 3.4 %copy-done = bf16[4096,1024]{1,0:T(8,128)(2,1)S(1)} copy-done((bf16[4096,1024]{1,0:T(8,128)(2,1)S(1)}, bf16[4096,1024]{1,0:T(8,128)(2,1)}, u32[]{:S(2)}) %copy-start) | copy-done | bytes 8388632
  10.9 6.8 %denominators.1 = (bf16[272,1024]{1,0:T(8,128)(2,1)S(1)}, bf16[272,1024]{1,0:T(8,128)(2,1)S(1)}, bf16[1024,1024]{1,0:T(8,128)(2,1)S(1)}, f32[8,1,128]{2,1,0:T(1,128)S(1)}) custom-call(bf16[4096,1024]{1,0:T(8,128)(2,1)S(1)} %copy-done, f32[8,1,512]{2,1,0:T(1,128)S(1)} %bitcast.5, bf16[4096,1024]{1,0:T(8,128)(2,1)S(1)} %copy-done, f32[32,1,128]{2,1,0:T(1,128)S(1)} %bitcast.6, ...), custom_call_target="tpu_custom_call" | custom-call | flops 4294967296 | bytes 9437184 | tf_op jit(solution)/shard_map/denominators/pallas_call | solution.py:121
  18.6 1.7 %collective-permute-start.3 = (bf16[256,1024]{1,0:T(8,128)(2,1)S(1)}, bf16[256,1024]{1,0:T(8,128)(2,1)S(1)}, u32[]{:S(2)}, u32[]{:S(2)}) collective-permute-start(bf16[256,1024]{1,0:T(8,128)(2,1)S(1)} %collective-permute-done.2.refs_0_.refs_9_.refs_7_), channel_id=1, source_target_pairs={{0,2},{1,3},{2,0},{3,1},{4,6},{5,7},{6,4},{7,5},{8,10},{9,11},{10,... | collective-permute-start | bytes 1572872 | tf_op jit(solution)/shard_map/ppermute | solution.py:330
  20.2 1.6 %collective-permute-start.5 = (bf16[256,1024]{1,0:T(8,128)(2,1)S(1)}, bf16[256,1024]{1,0:T(8,128)(2,1)S(1)}, u32[]{:S(2)}, u32[]{:S(2)}) collective-permute-start(bf16[256,1024]{1,0:T(8,128)(2,1)S(1)} %collective-permute-done.4.refs_1_.refs_8_.refs_6_), channel_id=1, source_target_pairs={{0,8},{1,9},{2,10},{3,11},{4,12},{5,13},{6,14},{7,15},{8,0},{9,1},... | collective-permute-start | bytes 1572872 | tf_op jit(solution)/shard_map/ppermute | solution.py:330
  21.8 2.5 %sums.5 = (f32[1024,1024]{1,0:T(8,128)S(1)}, f32[1024,128]{1,0:T(8,128)S(1)}) custom-call(bf16[1024,1024]{1,0:T(8,128)(2,1)S(1)} %get-tuple-element.56.c_ref, f32[8,1,128]{2,1,0:T(1,128)S(1)} %get-tuple-element.57.lw_ref, bf16[272,1024]{1,0:T(8,128)(2,1)S(1)} %get-tuple-element.59.tail_ref.refs_0_.refs_5_, ...), custom_call_target="tpu_custom_call" | custom-call | flops 2147483648 | bytes 3145728 | tf_op jit(solution)/shard_map/sums/pallas_call | solution.py:202
  24.4 9.0 %collective-permute-done.tail_ref.refs_1_.refs_10_.refs_8_ = bf16[272,1024]{1,0:T(8,128)(2,1)S(1)} collective-permute-done((bf16[272,1024]{1,0:T(8,128)(2,1)S(1)}, bf16[272,1024]{1,0:T(8,128)(2,1)S(1)}, u32[]{:S(2)}, u32[]{:S(2)}) %collective-permute-start) | collective-permute-done | bytes 557088 | tf_op jit(solution)/shard_map/ppermute | solution.py:330
  33.9 2.7 %sums.6 = (f32[1024,1024]{1,0:T(8,128)S(1)}, f32[1024,128]{1,0:T(8,128)S(1)}) custom-call(bf16[1024,1024]{1,0:T(8,128)(2,1)S(1)} %get-tuple-element.56.c_ref, f32[8,1,128]{2,1,0:T(1,128)S(1)} %get-tuple-element.57.lw_ref, bf16[272,1024]{1,0:T(8,128)(2,1)S(1)} %collective-permute-done.6.tail_ref.refs_0_.refs_7_.refs_5_, ...), custom_call_target="tpu_custom_call", output_to_operand_aliasing={{0}: (5, {}), {1}: (6, {})} | custom-call | flops 2147483648 | bytes 3145728 | tf_op jit(solution)/shard_map/sums/pallas_call | solution.py:202
  36.6 2.7 %sums.7 = (f32[1024,1024]{1,0:T(8,128)S(1)}, f32[1024,128]{1,0:T(8,128)S(1)}) custom-call(bf16[1024,1024]{1,0:T(8,128)(2,1)S(1)} %get-tuple-element.56.c_ref, f32[8,1,128]{2,1,0:T(1,128)S(1)} %get-tuple-element.57.lw_ref, bf16[272,1024]{1,0:T(8,128)(2,1)S(1)} %collective-permute-done.tail_ref.refs_1_.refs_10_.refs_8_, ...), custom_call_target="tpu_custom_call", output_to_operand_aliasing={{0}: (5, {}), {1}: (6, {})} | custom-call | flops 2147483648 | bytes 3145728 | tf_op jit(solution)/shard_map/sums/pallas_call | solution.py:202
  39.4 4.3 %collective-permute-done.1.tail_ref = bf16[16,1024]{1,0:T(8,128)(2,1)S(1)} collective-permute-done((bf16[16,1024]{1,0:T(8,128)(2,1)S(1)}, bf16[16,1024]{1,0:T(8,128)(2,1)S(1)}, u32[]{:S(2)}, u32[]{:S(2)}) %collective-permute-start.1) | collective-permute-done | bytes 32800 | tf_op jit(solution)/shard_map/ppermute | solution.py:330
  48.1 1.5 %collective-permute-start.10 = (bf16[64,1024]{1,0:T(8,128)(2,1)S(1)}, bf16[64,1024]{1,0:T(8,128)(2,1)S(1)}, u32[]{:S(2)}, u32[]{:S(2)}) collective-permute-start(bf16[64,1024]{1,0:T(8,128)(2,1)S(1)} %get-tuple-element.71), channel_id=1, source_target_pairs={{0,4},{1,5},{2,6},{3,7},{4,0},{5,1},{6,2},{7,3},{8,12},{9,13},{10,... | collective-permute-start | bytes 393224 | tf_op jit(solution)/shard_map/ppermute | solution.py:330
  50.2 4.3 %collective-permute-done.10.refs_2_ = bf16[64,1024]{1,0:T(8,128)(2,1)S(1)} collective-permute-done((bf16[64,1024]{1,0:T(8,128)(2,1)S(1)}, bf16[64,1024]{1,0:T(8,128)(2,1)S(1)}, u32[]{:S(2)}, u32[]{:S(2)}) %collective-permute-start.10) | collective-permute-done | bytes 131104 | tf_op jit(solution)/shard_map/ppermute | solution.py:330
  54.5 1.6 %collective-permute-start.15 = (f32[8,128]{1,0:T(8,128)S(1)}, f32[8,128]{1,0:T(8,128)S(1)}, u32[]{:S(2)}, u32[]{:S(2)}) collective-permute-start(f32[8,128]{1,0:T(8,128)S(1)} %maximum_add_fusion), channel_id=1, source_target_pairs={{0,4},{1,5},{2,6},{3,7},{4,0},{5,1},{6,2},{7,3},{8,12},{9,13},{10,... | collective-permute-start | bytes 12296 | tf_op jit(solution)/shard_map/ppermute | solution.py:330
  56.5 2.6 %collective-permute-start.11 = (bf16[64,1024]{1,0:T(8,128)(2,1)S(1)}, bf16[64,1024]{1,0:T(8,128)(2,1)S(1)}, u32[]{:S(2)}, u32[]{:S(2)}) collective-permute-start(bf16[64,1024]{1,0:T(8,128)(2,1)S(1)} %merge.4), channel_id=1, source_target_pairs={{0,16},{1,17},{2,18},{3,19},{4,20},{5,21},{6,22},{7,23},{8,24},{9,... | collective-permute-start | bytes 393224 | tf_op jit(solution)/shard_map/ppermute | solution.py:330
  59.6 3.4 %collective-permute-done.9.refs_2_ = bf16[128,1024]{1,0:T(8,128)(2,1)S(1)} collective-permute-done((bf16[128,1024]{1,0:T(8,128)(2,1)S(1)}, bf16[128,1024]{1,0:T(8,128)(2,1)S(1)}, u32[]{:S(2)}, u32[]{:S(2)}) %collective-permute-start.9) | collective-permute-done | bytes 262176 | tf_op jit(solution)/shard_map/ppermute | solution.py:330
  63.0 5.1 %collective-permute-done.11.refs_3_ = bf16[64,1024]{1,0:T(8,128)(2,1)S(1)} collective-permute-done((bf16[64,1024]{1,0:T(8,128)(2,1)S(1)}, bf16[64,1024]{1,0:T(8,128)(2,1)S(1)}, u32[]{:S(2)}, u32[]{:S(2)}) %collective-permute-start.11) | collective-permute-done | bytes 131104 | tf_op jit(solution)/shard_map/ppermute | solution.py:330
  68.4 2.8 %collective-permute-start.17 = (bf16[64,1024]{1,0:T(8,128)(2,1)S(1)}, bf16[64,1024]{1,0:T(8,128)(2,1)}, u32[]{:S(2)}, u32[]{:S(2)}) collective-permute-start(bf16[64,1024]{1,0:T(8,128)(2,1)S(1)} %directions.2.refs_0_), channel_id=1, source_target_pairs={{0,16},{1,17},{2,18},{3,19},{4,20},{5,21},{6,22},{7,23},{8,24},{9,... | collective-permute-start | bytes 393224 | tf_op jit(solution)/shard_map/ppermute | solution.py:330
  72.9 1.5 %collective-permute-start.22 = (bf16[64,1024]{1,0:T(8,128)(2,1)S(1)}, bf16[64,1024]{1,0:T(8,128)(2,1)}, u32[]{:S(2)}, u32[]{:S(2)}) collective-permute-start(bf16[64,1024]{1,0:T(8,128)(2,1)S(1)} %directions.3.refs_1_), channel_id=1, source_target_pairs={{0,4},{1,5},{2,6},{3,7},{4,0},{5,1},{6,2},{7,3},{8,12},{9,13},{10,... | collective-permute-start | bytes 393224 | tf_op jit(solution)/shard_map/ppermute | solution.py:330
  77.1 2.7 %normalizers.5 = (f32[1,512]{1,0:T(1,128)S(1)}, f32[1,512]{1,0:T(1,128)S(1)}, f32[1,512]{1,0:T(1,128)S(1)}, f32[1,512]{1,0:T(1,128)S(1)}) custom-call(bf16[64,1024]{1,0:T(8,128)(2,1)S(1)} %directions.2.refs_0_, bf16[64,1024]{1,0:T(8,128)(2,1)S(1)} %directions.3.refs_1_, bf16[64,1024]{1,0:T(8,128)(2,1)} %collective-permute-done.18.refs_2_, ...), custom_call_target="tpu_custom_call" | custom-call | flops 1073741824 | bytes 4718592 | tf_op jit(solution)/shard_map/normalizers/pallas_call | solution.py:303
  79.8 1.7 %collective-permute-done.17.refs_0_ = bf16[64,1024]{1,0:T(8,128)(2,1)} collective-permute-done((bf16[64,1024]{1,0:T(8,128)(2,1)S(1)}, bf16[64,1024]{1,0:T(8,128)(2,1)}, u32[]{:S(2)}, u32[]{:S(2)}) %collective-permute-start.17) | collective-permute-done | bytes 131104 | tf_op jit(solution)/shard_map/ppermute | solution.py:330
  82.1 1.5 %collective-permute-start.20 = (bf16[64,1024]{1,0:T(8,128)(2,1)}, bf16[64,1024]{1,0:T(8,128)(2,1)S(1)}, u32[]{:S(2)}, u32[]{:S(2)}) collective-permute-start(bf16[64,1024]{1,0:T(8,128)(2,1)} %collective-permute-done.17.refs_0_), channel_id=1, source_target_pairs={{0,4},{1,5},{2,6},{3,7},{4,0},{5,1},{6,2},{7,3},{8,12},{9,13},{10,... | collective-permute-start | bytes 393224 | tf_op jit(solution)/shard_map/ppermute | solution.py:330
  86.2 2.4 %normalizers.6 = (f32[1,512]{1,0:T(1,128)S(1)}, f32[1,512]{1,0:T(1,128)S(1)}, f32[1,512]{1,0:T(1,128)S(1)}, f32[1,512]{1,0:T(1,128)S(1)}) custom-call(bf16[64,1024]{1,0:T(8,128)(2,1)S(1)} %collective-permute-done.21.refs_0_, bf16[64,1024]{1,0:T(8,128)(2,1)} %collective-permute-done.22.refs_1_, bf16[64,1024]{1,0:T(8,128)(2,1)S(1)} %collective-permute-done.23.refs_2_, ...), custom_call_target="tpu_custom_call" | custom-call | flops 1073741824 | bytes 4718592 | tf_op jit(solution)/shard_map/normalizers/pallas_call | solution.py:303
  88.9 2.4 %normalizers.7 = (f32[1,512]{1,0:T(1,128)S(1)}, f32[1,512]{1,0:T(1,128)S(1)}, f32[1,512]{1,0:T(1,128)S(1)}, f32[1,512]{1,0:T(1,128)S(1)}) custom-call(bf16[64,1024]{1,0:T(8,128)(2,1)} %collective-permute-done.17.refs_0_, bf16[64,1024]{1,0:T(8,128)(2,1)} %collective-permute-done.25.refs_1_, bf16[64,1024]{1,0:T(8,128)(2,1)S(1)} %collective-permute-done.26.refs_2_, ...), custom_call_target="tpu_custom_call" | custom-call | flops 1073741824 | bytes 4718592 | tf_op jit(solution)/shard_map/normalizers/pallas_call | solution.py:303
  (89 shorter events, 26.6 us)
Async XLA Ops:
  2.2 18.1 %collective-permute-start.4 = (bf16[256,1024]{1,0:T(8,128)(2,1)S(1)}, bf16[256,1024]{1,0:T(8,128)(2,1)S(1)}, u32[]{:S(2)}, u32[]{:S(2)}) collective-permute-start(bf16[256,1024]{1,0:T(8,128)(2,1)S(1)} %get-tuple-element.55.b_ref), channel_id=1, source_target_pairs={{0,2},{1,3},{2,0},{3,1},{4,6},{5,7},{6,4},{7,5},{8,10},{9,11},{10,... | collective-permute-start | bytes 1572872 | tf_op jit(solution)/shard_map/ppermute | solution.py:330
  5.2 13.4 %collective-permute-start.2 = (bf16[256,1024]{1,0:T(8,128)(2,1)S(1)}, bf16[256,1024]{1,0:T(8,128)(2,1)S(1)}, u32[]{:S(2)}, u32[]{:S(2)}) collective-permute-start(bf16[256,1024]{1,0:T(8,128)(2,1)S(1)} %get-tuple-element.54.a_ref), channel_id=1, source_target_pairs={{0,8},{1,9},{2,10},{3,11},{4,12},{5,13},{6,14},{7,15},{8,0},{9,1},... | collective-permute-start | bytes 1572872 | tf_op jit(solution)/shard_map/ppermute | solution.py:330
  17.7 15.6 %collective-permute-start = (bf16[272,1024]{1,0:T(8,128)(2,1)S(1)}, bf16[272,1024]{1,0:T(8,128)(2,1)S(1)}, u32[]{:S(2)}, u32[]{:S(2)}) collective-permute-start(bf16[272,1024]{1,0:T(8,128)(2,1)S(1)} %get-tuple-element.58.refs_1_.refs_6_), channel_id=1, source_target_pairs={{0,8},{1,9},{2,10},{3,11},{4,12},{5,13},{6,14},{7,15},{8,0},{9,1},... | collective-permute-start | bytes 1671176 | tf_op jit(solution)/shard_map/ppermute | solution.py:330
  18.2 15.7 %collective-permute-start.6 = (bf16[272,1024]{1,0:T(8,128)(2,1)S(1)}, bf16[272,1024]{1,0:T(8,128)(2,1)S(1)}, u32[]{:S(2)}, u32[]{:S(2)}) collective-permute-start(bf16[272,1024]{1,0:T(8,128)(2,1)S(1)} %get-tuple-element.59.tail_ref.refs_0_.refs_5_), channel_id=1, source_target_pairs={{0,2},{1,3},{2,0},{3,1},{4,6},{5,7},{6,4},{7,5},{8,10},{9,11},{10,... | collective-permute-start | bytes 1671176 | tf_op jit(solution)/shard_map/ppermute | solution.py:330
  18.6 25.1 %collective-permute-start.3 = (bf16[256,1024]{1,0:T(8,128)(2,1)S(1)}, bf16[256,1024]{1,0:T(8,128)(2,1)S(1)}, u32[]{:S(2)}, u32[]{:S(2)}) collective-permute-start(bf16[256,1024]{1,0:T(8,128)(2,1)S(1)} %collective-permute-done.2.refs_0_.refs_9_.refs_7_), channel_id=1, source_target_pairs={{0,2},{1,3},{2,0},{3,1},{4,6},{5,7},{6,4},{7,5},{8,10},{9,11},{10,... | collective-permute-start | bytes 1572872 | tf_op jit(solution)/shard_map/ppermute | solution.py:330
  20.2 23.4 %collective-permute-start.5 = (bf16[256,1024]{1,0:T(8,128)(2,1)S(1)}, bf16[256,1024]{1,0:T(8,128)(2,1)S(1)}, u32[]{:S(2)}, u32[]{:S(2)}) collective-permute-start(bf16[256,1024]{1,0:T(8,128)(2,1)S(1)} %collective-permute-done.4.refs_1_.refs_8_.refs_6_), channel_id=1, source_target_pairs={{0,8},{1,9},{2,10},{3,11},{4,12},{5,13},{6,14},{7,15},{8,0},{9,1},... | collective-permute-start | bytes 1572872 | tf_op jit(solution)/shard_map/ppermute | solution.py:330
  33.3 10.3 %collective-permute-start.1 = (bf16[16,1024]{1,0:T(8,128)(2,1)S(1)}, bf16[16,1024]{1,0:T(8,128)(2,1)S(1)}, u32[]{:S(2)}, u32[]{:S(2)}) collective-permute-start(bf16[16,1024]{1,0:T(8,128)(2,1)S(1)} %slice.80), channel_id=1, source_target_pairs={{0,2},{1,3},{2,0},{3,1},{4,6},{5,7},{6,4},{7,5},{8,10},{9,11},{10,... | collective-permute-start | bytes 98312 | tf_op jit(solution)/shard_map/ppermute | solution.py:330
  45.1 5.0 %collective-permute-start.7 = (f32[256,1024]{1,0:T(8,128)S(1)}, f32[256,1024]{1,0:T(8,128)S(1)}, u32[]{:S(2)}, u32[]{:S(2)}) collective-permute-start(f32[256,1024]{1,0:T(8,128)S(1)} %get-tuple-element.67), channel_id=1, source_target_pairs={{0,1},{1,0},{2,3},{3,2},{4,5},{5,4},{6,7},{7,6},{8,9},{9,8},{10,11... | collective-permute-start | bytes 3145736 | tf_op jit(solution)/shard_map/ppermute | solution.py:330
  48.1 6.3 %collective-permute-start.10 = (bf16[64,1024]{1,0:T(8,128)(2,1)S(1)}, bf16[64,1024]{1,0:T(8,128)(2,1)S(1)}, u32[]{:S(2)}, u32[]{:S(2)}) collective-permute-start(bf16[64,1024]{1,0:T(8,128)(2,1)S(1)} %get-tuple-element.71), channel_id=1, source_target_pairs={{0,4},{1,5},{2,6},{3,7},{4,0},{5,1},{6,2},{7,3},{8,12},{9,13},{10,... | collective-permute-start | bytes 393224 | tf_op jit(solution)/shard_map/ppermute | solution.py:330
  49.6 9.5 %collective-permute-start.12 = (bf16[64,1024]{1,0:T(8,128)(2,1)S(1)}, bf16[64,1024]{1,0:T(8,128)(2,1)S(1)}, u32[]{:S(2)}, u32[]{:S(2)}) collective-permute-start(bf16[64,1024]{1,0:T(8,128)(2,1)S(1)} %get-tuple-element.72), channel_id=1, source_target_pairs={{0,4},{1,5},{2,6},{3,7},{4,0},{5,1},{6,2},{7,3},{8,12},{9,13},{10,... | collective-permute-start | bytes 393224 | tf_op jit(solution)/shard_map/ppermute | solution.py:330
  54.5 5.1 %collective-permute-start.15 = (f32[8,128]{1,0:T(8,128)S(1)}, f32[8,128]{1,0:T(8,128)S(1)}, u32[]{:S(2)}, u32[]{:S(2)}) collective-permute-start(f32[8,128]{1,0:T(8,128)S(1)} %maximum_add_fusion), channel_id=1, source_target_pairs={{0,4},{1,5},{2,6},{3,7},{4,0},{5,1},{6,2},{7,3},{8,12},{9,13},{10,... | collective-permute-start | bytes 12296 | tf_op jit(solution)/shard_map/ppermute | solution.py:330
  56.0 7.0 %collective-permute-start.9 = (bf16[128,1024]{1,0:T(8,128)(2,1)S(1)}, bf16[128,1024]{1,0:T(8,128)(2,1)S(1)}, u32[]{:S(2)}, u32[]{:S(2)}) collective-permute-start(bf16[128,1024]{1,0:T(8,128)(2,1)S(1)} %get-tuple-element.70), channel_id=1, source_target_pairs={{0,4},{1,5},{2,6},{3,7},{4,0},{5,1},{6,2},{7,3},{8,12},{9,13},{10,... | collective-permute-start | bytes 786440 | tf_op jit(solution)/shard_map/ppermute | solution.py:330
  56.5 11.5 %collective-permute-start.11 = (bf16[64,1024]{1,0:T(8,128)(2,1)S(1)}, bf16[64,1024]{1,0:T(8,128)(2,1)S(1)}, u32[]{:S(2)}, u32[]{:S(2)}) collective-permute-start(bf16[64,1024]{1,0:T(8,128)(2,1)S(1)} %merge.4), channel_id=1, source_target_pairs={{0,16},{1,17},{2,18},{3,19},{4,20},{5,21},{6,22},{7,23},{8,24},{9,... | collective-permute-start | bytes 393224 | tf_op jit(solution)/shard_map/ppermute | solution.py:330
  59.2 12.1 %collective-permute-start.13 = (bf16[64,1024]{1,0:T(8,128)(2,1)S(1)}, bf16[64,1024]{1,0:T(8,128)(2,1)S(1)}, u32[]{:S(2)}, u32[]{:S(2)}) collective-permute-start(bf16[64,1024]{1,0:T(8,128)(2,1)S(1)} %merge.5), channel_id=1, source_target_pairs={{0,16},{1,17},{2,18},{3,19},{4,20},{5,21},{6,22},{7,23},{8,24},{9,... | collective-permute-start | bytes 393224 | tf_op jit(solution)/shard_map/ppermute | solution.py:330
  68.2 4.6 %collective-permute-start.16 = (f32[8,128]{1,0:T(8,128)S(1)}, f32[8,128]{1,0:T(8,128)S(1)}, u32[]{:S(2)}, u32[]{:S(2)}) collective-permute-start(f32[8,128]{1,0:T(8,128)S(1)} %maximum_add_fusion.1), channel_id=1, source_target_pairs={{0,16},{1,17},{2,18},{3,19},{4,20},{5,21},{6,22},{7,23},{8,24},{9,... | collective-permute-start | bytes 12296 | tf_op jit(solution)/shard_map/ppermute | solution.py:330
  68.3 6.7 %collective-permute-start.18 = (bf16[64,1024]{1,0:T(8,128)(2,1)S(1)}, bf16[64,1024]{1,0:T(8,128)(2,1)}, u32[]{:S(2)}, u32[]{:S(2)}) collective-permute-start(bf16[64,1024]{1,0:T(8,128)(2,1)S(1)} %directions.2.refs_0_), channel_id=1, source_target_pairs={{0,1},{1,0},{2,3},{3,2},{4,5},{5,4},{6,7},{7,6},{8,9},{9,8},{10,11... | collective-permute-start | bytes 393224 | tf_op jit(solution)/shard_map/ppermute | solution.py:330
  68.4 13.1 %collective-permute-start.17 = (bf16[64,1024]{1,0:T(8,128)(2,1)S(1)}, bf16[64,1024]{1,0:T(8,128)(2,1)}, u32[]{:S(2)}, u32[]{:S(2)}) collective-permute-start(bf16[64,1024]{1,0:T(8,128)(2,1)S(1)} %directions.2.refs_0_), channel_id=1, source_target_pairs={{0,16},{1,17},{2,18},{3,19},{4,20},{5,21},{6,22},{7,23},{8,24},{9,... | collective-permute-start | bytes 393224 | tf_op jit(solution)/shard_map/ppermute | solution.py:330
  71.7 12.3 %collective-permute-start.25 = (bf16[64,1024]{1,0:T(8,128)(2,1)S(1)}, bf16[64,1024]{1,0:T(8,128)(2,1)}, u32[]{:S(2)}, u32[]{:S(2)}) collective-permute-start(bf16[64,1024]{1,0:T(8,128)(2,1)S(1)} %directions.3.refs_1_), channel_id=1, source_target_pairs={{0,16},{1,17},{2,18},{3,19},{4,20},{5,21},{6,22},{7,23},{8,24},{9,... | collective-permute-start | bytes 393224 | tf_op jit(solution)/shard_map/ppermute | solution.py:330
  72.9 8.6 %collective-permute-start.22 = (bf16[64,1024]{1,0:T(8,128)(2,1)S(1)}, bf16[64,1024]{1,0:T(8,128)(2,1)}, u32[]{:S(2)}, u32[]{:S(2)}) collective-permute-start(bf16[64,1024]{1,0:T(8,128)(2,1)S(1)} %directions.3.refs_1_), channel_id=1, source_target_pairs={{0,4},{1,5},{2,6},{3,7},{4,0},{5,1},{6,2},{7,3},{8,12},{9,13},{10,... | collective-permute-start | bytes 393224 | tf_op jit(solution)/shard_map/ppermute | solution.py:330
  74.4 7.5 %collective-permute-start.21 = (bf16[64,1024]{1,0:T(8,128)(2,1)S(1)}, bf16[64,1024]{1,0:T(8,128)(2,1)S(1)}, u32[]{:S(2)}, u32[]{:S(2)}) collective-permute-start(bf16[64,1024]{1,0:T(8,128)(2,1)S(1)} %directions.2.refs_0_), channel_id=1, source_target_pairs={{0,4},{1,5},{2,6},{3,7},{4,0},{5,1},{6,2},{7,3},{8,12},{9,13},{10,... | collective-permute-start | bytes 393224 | tf_op jit(solution)/shard_map/ppermute | solution.py:330
  81.5 4.8 %collective-permute-start.24 = (bf16[64,1024]{1,0:T(8,128)(2,1)}, bf16[64,1024]{1,0:T(8,128)(2,1)S(1)}, u32[]{:S(2)}, u32[]{:S(2)}) collective-permute-start(bf16[64,1024]{1,0:T(8,128)(2,1)} %collective-permute-done.22.refs_1_), channel_id=1, source_target_pairs={{0,1},{1,0},{2,3},{3,2},{4,5},{5,4},{6,7},{7,6},{8,9},{9,8},{10,11... | collective-permute-start | bytes 393224 | tf_op jit(solution)/shard_map/ppermute | solution.py:330
  82.1 6.6 %collective-permute-start.20 = (bf16[64,1024]{1,0:T(8,128)(2,1)}, bf16[64,1024]{1,0:T(8,128)(2,1)S(1)}, u32[]{:S(2)}, u32[]{:S(2)}) collective-permute-start(bf16[64,1024]{1,0:T(8,128)(2,1)} %collective-permute-done.17.refs_0_), channel_id=1, source_target_pairs={{0,4},{1,5},{2,6},{3,7},{4,0},{5,1},{6,2},{7,3},{8,12},{9,13},{10,... | collective-permute-start | bytes 393224 | tf_op jit(solution)/shard_map/ppermute | solution.py:330
  84.0 5.0 %collective-permute-start.28 = (bf16[64,1024]{1,0:T(8,128)(2,1)}, bf16[64,1024]{1,0:T(8,128)(2,1)S(1)}, u32[]{:S(2)}, u32[]{:S(2)}) collective-permute-start(bf16[64,1024]{1,0:T(8,128)(2,1)} %collective-permute-done.25.refs_1_), channel_id=1, source_target_pairs={{0,1},{1,0},{2,3},{3,2},{4,5},{5,4},{6,7},{7,6},{8,9},{9,8},{10,11... | collective-permute-start | bytes 393224 | tf_op jit(solution)/shard_map/ppermute | solution.py:330
  84.7 6.7 %collective-permute-start.27 = (bf16[64,1024]{1,0:T(8,128)(2,1)}, bf16[64,1024]{1,0:T(8,128)(2,1)S(1)}, u32[]{:S(2)}, u32[]{:S(2)}) collective-permute-start(bf16[64,1024]{1,0:T(8,128)(2,1)} %collective-permute-done.25.refs_1_), channel_id=1, source_target_pairs={{0,4},{1,5},{2,6},{3,7},{4,0},{5,1},{6,2},{7,3},{8,12},{9,13},{10,... | collective-permute-start | bytes 393224 | tf_op jit(solution)/shard_map/ppermute | solution.py:330
  (18 other events, 86.2 us)
